TPU v7x, 32 devices: a whole 2x2x4 slice. The times are simulated.
32 devices in a mesh: dp: 8 (over z, y), fsdp: 4 (over x, core).
Axes of the slice: x: 2, y: 2, z: 4, core: 2. Of those that a mesh axis runs over, the one named last changes fastest.
Arguments:
- tokens: bfloat16 [32768, 768], P(('dp', 'fsdp')), may hold values from -6 to 6
- ends: int32 [32, 24], P(('dp', 'fsdp')), may hold values from 20 to 1023, as said below
- cot_out: bfloat16 [32768, 768], P(('dp', 'fsdp')), may hold values from -6 to 6
- cot_pooled: float32 [32, 24, 768], P(('dp', 'fsdp')), may hold values from -6 to 6
- w_qkv: float32 [768, 2304], P(('dp', 'fsdp')), may hold values from -0.21875 to 0.21875
- w_out: float32 [768, 768], P(('dp', 'fsdp')), may hold values from -1.25 to 1.25
- w_up: float32 [768, 3072], P(('dp', 'fsdp')), may hold values from -0.21875 to 0.21875
- w_down: float32 [3072, 768], P(('dp', 'fsdp')), may hold values from -0.109375 to 0.109375
- vectors: float32 [768, 8], P(('dp', 'fsdp')), may hold values from -1.5 to 4.8, as said below
- bias_up: float32 [3072], P(('dp', 'fsdp')), may hold values from -1.5 to 1.5
- row_qkv: float32 [768], P(('dp', 'fsdp')), may hold values from 6553.6 to 24576
- col_qkv: float32 [2304], replicated, may hold values from 6553.6 to 13107.2
- row_out: float32 [768], P(('dp', 'fsdp')), may hold values from 819.2 to 3276.8
- col_out: float32 [768], replicated, may hold values from 819.2 to 3276.8
- row_up: float32 [768], P(('dp', 'fsdp')), may hold values from 983.04 to 3604.48
- col_up: float32 [3072], replicated, may hold values from 983.04 to 1966.08
- row_down: float32 [3072], P(('dp', 'fsdp')), may hold values from 3604.48 to 14745.6
- col_down: float32 [768], replicated, may hold values from 3604.48 to 14745.6
- moment_vectors: float32 [768, 8], P(('dp', 'fsdp')), may hold values from 1638.4 to 16384
- moment_bias_up: float32 [3072], P(('dp', 'fsdp')), may hold values from 819.2 to 3276.8
Outputs:
- out_tokens: bfloat16 [32768, 768], P(('dp', 'fsdp'))
- pooled: float32 [32, 24, 768], P(('dp', 'fsdp'))
- grad_tokens: float32 [32768, 768], P(('dp', 'fsdp'))
- grad_w_qkv: float32 [768, 2304], P(('dp', 'fsdp'))
- new_row_qkv: float32 [768], P(('dp', 'fsdp'))
- new_col_qkv: float32 [2304], replicated
- new_w_qkv: float32 [768, 2304], P(('dp', 'fsdp'))
- grad_w_out: float32 [768, 768], P(('dp', 'fsdp'))
- new_row_out: float32 [768], P(('dp', 'fsdp'))
- new_col_out: float32 [768], replicated
- new_w_out: float32 [768, 768], P(('dp', 'fsdp'))
- grad_w_up: float32 [768, 3072], P(('dp', 'fsdp'))
- new_row_up: float32 [768], P(('dp', 'fsdp'))
- new_col_up: float32 [3072], replicated
- new_w_up: float32 [768, 3072], P(('dp', 'fsdp'))
- grad_w_down: float32 [3072, 768], P(('dp', 'fsdp'))
- new_row_down: float32 [3072], P(('dp', 'fsdp'))
- new_col_down: float32 [768], replicated
- new_w_down: float32 [3072, 768], P(('dp', 'fsdp'))
- grad_vectors: float32 [768, 8], P(('dp', 'fsdp'))
- new_moment_vectors: float32 [768, 8], P(('dp', 'fsdp'))
- new_vectors: float32 [768, 8], P(('dp', 'fsdp'))
- grad_bias_up: float32 [3072], P(('dp', 'fsdp'))
- new_moment_bias_up: float32 [3072], P(('dp', 'fsdp'))
- new_bias_up: float32 [3072], P(('dp', 'fsdp'))
- clip_scale: float32 [], replicated
Inputs may be any that keep to these rules, and one draw needn't show every extreme that they name: ends[r, s] is the last position of caption s of row r: they rise strictly along s, the last of each row is 1023, and each caption holds between 21 and 64 positions. `vectors`: columns 0 and 2 (the norms' gains) are positive; the other columns are biases of both signs.
All inputs are finite; a program needn't handle non-finite values.
Results may differ from a plain program's by a relative error of at most 0.01.
The roundings to bfloat16 on the way count: a program that leaves them out, or rounds other values in their place, can miss the bound.
Values may be sent and summed in bfloat16 or wider, within the bound.
A program may use at most 256 MiB of HBM per device.

v0:
```python
import jax
import jax.numpy as jnp
from jax import lax
from jax.sharding import PartitionSpec as P

D = 768
HEADS = 12
HEAD_DIM = 64
FF = 3072
SEQ = 1024
STEP = 10


norm_eps = 1e-06
square_eps = 1e-30
clip_limit = 1.0
step_rate = 0.5
scale_floor = 0.001
highest = lax.Precision.HIGHEST


def layer_norm(values, gain, shift):
    centre = jnp.mean(values, -1, keepdims=True)
    centred = values - centre
    spread = jnp.mean(centred * centred, -1, keepdims=True)
    return centred * lax.rsqrt(spread + norm_eps) * gain + shift


def gelu_tanh(values):
    return jax.nn.gelu(values, approximate=True)


def matmul(left, right):
    return jnp.dot(left, right, preferred_element_type=jnp.float32)


def matmul_tn(left, right):
    return lax.dot_general(
        left, right, (((0,), (0,)), ((), ())), preferred_element_type=jnp.float32
    )


def matmul_nt(left, right):
    return lax.dot_general(
        left, right, (((1,), (1,)), ((), ())), preferred_element_type=jnp.float32
    )


def segment_ids(ends_row):
    places = jnp.arange(SEQ, dtype=jnp.int32)
    return jnp.sum((places[:, None] > ends_row[None, :]).astype(jnp.int32), 1)


def masked_scores(query_block, key_heads, segment_block, segment):
    factor = HEAD_DIM ** (-0.5)
    scores = (
        jnp.einsum("qhd,khd->hqk", query_block, key_heads, preferred_element_type=jnp.float32)
        * factor
    )
    same = segment_block[:, None] == segment[None, :]
    return jnp.where(same[None], scores, -1e30)


def attend_row(entry):
    query_row, key_row, value_row, segment = entry
    block = min(512, SEQ)
    key_heads = key_row.reshape(SEQ, HEADS, HEAD_DIM)
    value_heads = value_row.reshape(SEQ, HEADS, HEAD_DIM)
    outputs, peaks, totals = ([], [], [])
    for offset in range(0, SEQ, block):
        query_block = query_row[offset : offset + block].reshape(block, HEADS, HEAD_DIM)
        scores = masked_scores(query_block, key_heads, segment[offset : offset + block], segment)
        peak = jnp.max(scores, -1, keepdims=True)
        expo = jnp.exp(scores - peak)
        total = jnp.sum(expo, -1, keepdims=True)
        probs = (expo / total).astype(jnp.bfloat16)
        mixed = jnp.einsum("hqk,khd->qhd", probs, value_heads, preferred_element_type=jnp.float32)
        outputs.append(mixed.reshape(block, HEADS * HEAD_DIM))
        peaks.append(peak)
        totals.append(total)
    return (jnp.concatenate(outputs, 0), jnp.concatenate(peaks, 1), jnp.concatenate(totals, 1))


def attend_back(entry):
    query_row, key_row, value_row, segment, grad_row, peaks, totals = entry
    block = min(512, SEQ)
    factor = HEAD_DIM ** (-0.5)
    key_heads = key_row.reshape(SEQ, HEADS, HEAD_DIM)
    value_heads = value_row.reshape(SEQ, HEADS, HEAD_DIM)
    grad_keys = jnp.zeros((SEQ, HEADS, HEAD_DIM), jnp.float32)
    grad_values = jnp.zeros((SEQ, HEADS, HEAD_DIM), jnp.float32)
    grad_queries = []
    for offset in range(0, SEQ, block):
        query_block = query_row[offset : offset + block].reshape(block, HEADS, HEAD_DIM)
        scores = masked_scores(query_block, key_heads, segment[offset : offset + block], segment)
        probs_full = (
            jnp.exp(scores - peaks[:, offset : offset + block]) / totals[:, offset : offset + block]
        )
        probs = probs_full.astype(jnp.bfloat16)
        grad_block = grad_row[offset : offset + block].reshape(block, HEADS, HEAD_DIM)
        grad_probs = jnp.einsum(
            "qhd,khd->hqk", grad_block, value_heads, preferred_element_type=jnp.float32
        )
        grad_scores = probs_full * (
            grad_probs - jnp.sum(probs_full * grad_probs, -1, keepdims=True)
        )
        grad_low = grad_scores.astype(jnp.bfloat16)
        grad_queries.append(
            jnp.einsum("hqk,khd->qhd", grad_low, key_heads, preferred_element_type=jnp.float32)
            * factor
        )
        grad_keys = (
            grad_keys
            + jnp.einsum("hqk,qhd->khd", grad_low, query_block, preferred_element_type=jnp.float32)
            * factor
        )
        grad_values = grad_values + jnp.einsum(
            "hqk,qhd->khd", probs, grad_block, preferred_element_type=jnp.float32
        )
    return (jnp.concatenate(grad_queries, 0), grad_keys, grad_values)


def per_device(
    tokens,
    ends,
    cot_out,
    cot_pooled,
    w_qkv,
    w_out,
    w_up,
    w_down,
    vectors,
    bias_up,
    row_qkv,
    col_qkv,
    row_out,
    col_out,
    row_up,
    col_up,
    row_down,
    col_down,
    moment_vectors,
    moment_bias_up,
):
    width = tokens.shape[1]
    row_count = ends.shape[0]
    low_qkv = w_qkv.astype(jnp.bfloat16)
    low_out = w_out.astype(jnp.bfloat16)
    low_up = w_up.astype(jnp.bfloat16)
    low_down = w_down.astype(jnp.bfloat16)
    low_vec = vectors.astype(jnp.bfloat16)
    low_upbias = bias_up.astype(jnp.bfloat16)
    gathered = (
        lax.all_gather(low_qkv, ("dp", "fsdp"), axis=0, tiled=True),
        lax.all_gather(low_out, ("dp", "fsdp"), axis=0, tiled=True),
        lax.all_gather(low_up, ("dp", "fsdp"), axis=0, tiled=True),
        lax.all_gather(low_down, ("dp", "fsdp"), axis=0, tiled=True),
        lax.all_gather(low_vec, ("dp", "fsdp"), axis=0, tiled=True),
        lax.all_gather(low_upbias, ("dp", "fsdp"), axis=0, tiled=True),
    )
    qkv_full, out_full, up_full, down_full = (gathered[0], gathered[1], gathered[2], gathered[3])
    vec_full = gathered[4].astype(jnp.float32)
    upbias_full = gathered[5].astype(jnp.float32)
    gain_one, shift_one, gain_two, shift_two = (
        vec_full[:, 0],
        vec_full[:, 1],
        vec_full[:, 2],
        vec_full[:, 3],
    )
    bias_query, bias_value, bias_attn, bias_down = (
        vec_full[:, 4],
        vec_full[:, 5],
        vec_full[:, 6],
        vec_full[:, 7],
    )
    inputs = tokens.astype(jnp.float32)
    segments = jax.vmap(segment_ids)(ends)
    normed_one = layer_norm(inputs, gain_one, shift_one)
    normed_low = normed_one.astype(jnp.bfloat16)
    projected = matmul(normed_low, qkv_full)
    queries = (projected[:, :width] + bias_query).astype(jnp.bfloat16)
    keys_low = projected[:, width : 2 * width].astype(jnp.bfloat16)
    values_low = (projected[:, 2 * width :] + bias_value).astype(jnp.bfloat16)
    row_queries = queries.reshape(row_count, SEQ, width)
    row_keys = keys_low.reshape(row_count, SEQ, width)
    row_values = values_low.reshape(row_count, SEQ, width)
    attended, peaks, totals = lax.map(attend_row, (row_queries, row_keys, row_values, segments))
    attended_low = attended.reshape(row_count * SEQ, width).astype(jnp.bfloat16)
    middle = inputs + (matmul(attended_low, out_full) + bias_attn)
    normed_two = layer_norm(middle, gain_two, shift_two)
    normed_two_low = normed_two.astype(jnp.bfloat16)
    hidden_pre = matmul(normed_two_low, up_full) + upbias_full
    hidden_low = gelu_tanh(hidden_pre).astype(jnp.bfloat16)
    final = middle + (matmul(hidden_low, down_full) + bias_down)
    picker = (jnp.arange(SEQ, dtype=jnp.int32)[None, None, :] == ends[:, :, None]).astype(
        jnp.float32
    )
    pooled = jnp.einsum(
        "rst,rtd->rsd",
        picker,
        final.reshape(row_count, SEQ, width),
        precision=highest,
        preferred_element_type=jnp.float32,
    )
    again = (
        lax.all_gather(low_qkv, ("dp", "fsdp"), axis=0, tiled=True),
        lax.all_gather(low_out, ("dp", "fsdp"), axis=0, tiled=True),
        lax.all_gather(low_up, ("dp", "fsdp"), axis=0, tiled=True),
        lax.all_gather(low_down, ("dp", "fsdp"), axis=0, tiled=True),
        lax.all_gather(low_vec, ("dp", "fsdp"), axis=0, tiled=True),
        lax.all_gather(low_upbias, ("dp", "fsdp"), axis=0, tiled=True),
    )
    qkv_back, out_back, up_back, down_back = (again[0], again[1], again[2], again[3])
    pooled_back = jnp.einsum(
        "rst,rsd->rtd", picker, cot_pooled, precision=highest, preferred_element_type=jnp.float32
    )
    grad_final = cot_out.astype(jnp.float32) + pooled_back.reshape(row_count * SEQ, width)
    grad_branch = grad_final.astype(jnp.bfloat16)
    grad_w_down = matmul_tn(hidden_low, grad_branch)
    grad_bias_down = jnp.sum(grad_branch.astype(jnp.float32), 0)
    grad_hidden = matmul_nt(grad_branch, down_back)
    gelu_pull = jax.vjp(gelu_tanh, hidden_pre)[1]
    grad_pre = gelu_pull(grad_hidden)[0].astype(jnp.bfloat16)
    grad_bias_up = jnp.sum(grad_pre.astype(jnp.float32), 0)
    grad_w_up = matmul_tn(normed_two_low, grad_pre)
    grad_normed_two = matmul_nt(grad_pre, up_back)
    norm_two_pull = jax.vjp(layer_norm, middle, gain_two, shift_two)[1]
    grad_mid_norm, grad_gain_two, grad_shift_two = norm_two_pull(grad_normed_two)
    grad_middle = grad_final + grad_mid_norm
    summed_up, summed_down, summed_upbias = (
        lax.psum_scatter(grad_w_up, ("dp", "fsdp"), scatter_dimension=0, tiled=True),
        lax.psum_scatter(grad_w_down, ("dp", "fsdp"), scatter_dimension=0, tiled=True),
        lax.psum_scatter(grad_bias_up, ("dp", "fsdp"), scatter_dimension=0, tiled=True),
    )
    grad_attn = grad_middle.astype(jnp.bfloat16)
    grad_w_out = matmul_tn(attended_low, grad_attn)
    grad_bias_attn = jnp.sum(grad_attn.astype(jnp.float32), 0)
    grad_attended = matmul_nt(grad_attn, out_back).astype(jnp.bfloat16)
    grad_q, grad_k, grad_v = lax.map(
        attend_back,
        (
            row_queries,
            row_keys,
            row_values,
            segments,
            grad_attended.reshape(row_count, SEQ, width),
            peaks,
            totals,
        ),
    )
    token_count = row_count * SEQ
    grad_proj = jnp.concatenate(
        [
            grad_q.reshape(token_count, width),
            grad_k.reshape(token_count, width),
            grad_v.reshape(token_count, width),
        ],
        1,
    ).astype(jnp.bfloat16)
    grad_bias_query = jnp.sum(grad_proj[:, :width].astype(jnp.float32), 0)
    grad_bias_value = jnp.sum(grad_proj[:, 2 * width :].astype(jnp.float32), 0)
    grad_w_qkv = matmul_tn(normed_low, grad_proj)
    grad_normed_one = matmul_nt(grad_proj, qkv_back)
    norm_one_pull = jax.vjp(layer_norm, inputs, gain_one, shift_one)[1]
    grad_in_norm, grad_gain_one, grad_shift_one = norm_one_pull(grad_normed_one)
    grad_tokens = grad_middle + grad_in_norm
    grad_vectors = jnp.stack(
        [
            grad_gain_one,
            grad_shift_one,
            grad_gain_two,
            grad_shift_two,
            grad_bias_query,
            grad_bias_value,
            grad_bias_attn,
            grad_bias_down,
        ],
        1,
    )
    summed_qkv, summed_out, summed_vec = (
        lax.psum_scatter(grad_w_qkv, ("dp", "fsdp"), scatter_dimension=0, tiled=True),
        lax.psum_scatter(grad_w_out, ("dp", "fsdp"), scatter_dimension=0, tiled=True),
        lax.psum_scatter(grad_vectors, ("dp", "fsdp"), scatter_dimension=0, tiled=True),
    )
    decay = 1.0 - STEP ** (-0.8)
    matrices = (summed_qkv, summed_out, summed_up, summed_down)
    old_rows = (row_qkv, row_out, row_up, row_down)
    old_cols = (col_qkv, col_out, col_up, col_down)
    masters = (w_qkv, w_out, w_up, w_down)
    row_sizes = (D, D, D, FF)
    tensor_sizes = (3 * D * D, D * D, D * FF, FF * D)
    squares = [gradient * gradient + square_eps for gradient in matrices]
    rows_new = [
        decay * old + (1.0 - decay) * jnp.mean(square, 1) for old, square in zip(old_rows, squares)
    ]
    col_parts = [jnp.sum(square, 0) for square in squares]
    local_totals = jnp.concatenate(
        [
            jnp.stack([jnp.sum(renewed) for renewed in rows_new]),
            jnp.stack([jnp.sum(master * master) for master in masters]),
            jnp.sum(vectors * vectors, 0),
            jnp.sum(bias_up * bias_up)[None],
        ]
    )
    col_sum_qkv, col_sum_out, col_sum_up, col_sum_down, global_totals = lax.psum(
        (col_parts[0], col_parts[1], col_parts[2], col_parts[3], local_totals), ("dp", "fsdp")
    )
    col_sums = (col_sum_qkv, col_sum_out, col_sum_up, col_sum_down)
    cols_new = [
        decay * old + (1.0 - decay) * (summed / count)
        for old, summed, count in zip(old_cols, col_sums, row_sizes)
    ]
    updates = []
    for index_mat in range(4):
        row_mean = global_totals[index_mat] / row_sizes[index_mat]
        renewed_row = rows_new[index_mat]
        renewed_col = cols_new[index_mat]
        updates.append(
            matrices[index_mat] * lax.rsqrt(renewed_row[:, None] * renewed_col[None, :] / row_mean)
        )
    moment_vec = decay * moment_vectors + (1.0 - decay) * (summed_vec * summed_vec + square_eps)
    update_vec = summed_vec * lax.rsqrt(moment_vec)
    moment_upb = decay * moment_bias_up + (1.0 - decay) * (
        summed_upbias * summed_upbias + square_eps
    )
    update_upb = summed_upbias * lax.rsqrt(moment_upb)
    local_norm = jnp.sum(update_vec * update_vec) + jnp.sum(update_upb * update_upb)
    for update in updates:
        local_norm = local_norm + jnp.sum(update * update)
    norm_total = lax.psum(local_norm, ("dp", "fsdp"))
    param_count = 4 * D * D + 2 * D * FF + 8 * D + FF
    clip = jnp.maximum(1.0, jnp.sqrt(norm_total / param_count) / clip_limit)
    new_weights = []
    for index_mat in range(4):
        scale = jnp.maximum(
            scale_floor, jnp.sqrt(global_totals[4 + index_mat] / tensor_sizes[index_mat])
        )
        new_weights.append(masters[index_mat] - step_rate * scale * updates[index_mat] / clip)
    vec_scale = jnp.maximum(scale_floor, jnp.sqrt(global_totals[8:16] / D))[None, :]
    new_vec = vectors - step_rate * vec_scale * update_vec / clip
    upb_scale = jnp.maximum(scale_floor, jnp.sqrt(global_totals[16] / FF))
    new_upb = bias_up - step_rate * upb_scale * update_upb / clip
    return (
        final.astype(jnp.bfloat16),
        pooled,
        grad_tokens,
        summed_qkv,
        rows_new[0],
        cols_new[0],
        new_weights[0],
        summed_out,
        rows_new[1],
        cols_new[1],
        new_weights[1],
        summed_up,
        rows_new[2],
        cols_new[2],
        new_weights[2],
        summed_down,
        rows_new[3],
        cols_new[3],
        new_weights[3],
        summed_vec,
        moment_vec,
        new_vec,
        summed_upbias,
        moment_upb,
        new_upb,
        clip,
    )


def solution(mesh):
    in_specs = (
        P(("dp", "fsdp"), None),
        P(("dp", "fsdp"), None),
        P(("dp", "fsdp"), None),
        P(("dp", "fsdp"), None, None),
        P(("dp", "fsdp"), None),
        P(("dp", "fsdp"), None),
        P(("dp", "fsdp"), None),
        P(("dp", "fsdp"), None),
        P(("dp", "fsdp"), None),
        P(("dp", "fsdp")),
        P(("dp", "fsdp")),
        P(),
        P(("dp", "fsdp")),
        P(),
        P(("dp", "fsdp")),
        P(),
        P(("dp", "fsdp")),
        P(),
        P(("dp", "fsdp"), None),
        P(("dp", "fsdp")),
    )
    out_specs = (
        P(("dp", "fsdp"), None),
        P(("dp", "fsdp"), None, None),
        P(("dp", "fsdp"), None),
        P(("dp", "fsdp"), None),
        P(("dp", "fsdp")),
        P(),
        P(("dp", "fsdp"), None),
        P(("dp", "fsdp"), None),
        P(("dp", "fsdp")),
        P(),
        P(("dp", "fsdp"), None),
        P(("dp", "fsdp"), None),
        P(("dp", "fsdp")),
        P(),
        P(("dp", "fsdp"), None),
        P(("dp", "fsdp"), None),
        P(("dp", "fsdp")),
        P(),
        P(("dp", "fsdp"), None),
        P(("dp", "fsdp"), None),
        P(("dp", "fsdp"), None),
        P(("dp", "fsdp"), None),
        P(("dp", "fsdp")),
        P(("dp", "fsdp")),
        P(("dp", "fsdp")),
        P(),
    )
    return jax.shard_map(
        per_device, mesh=mesh, in_specs=in_specs, out_specs=out_specs, check_vma=False
    )
```

profile of v0, /device:TPU:0, one launch (start us, length us, event | category | flops | bytes accessed | tf_op | source)
XLA Modules:
  0.0 1017.3 jit_solution(13640285331263873981)
XLA Ops:
  7.3 2.4 multiply_reduce_fusion.10
  9.8 2.2 multiply_reduce_fusion.12
  12.0 2.4 multiply_reduce_fusion.8
  14.5 2.3 multiply_reduce_fusion.7
  20.6 42.6 %all-reduce = bf16[3072]{0:T(1024)(128)(2,1)S(1)} all-reduce(bf16[3072]{0:T(1024)(128)(2,1)S(1)} %dynamic-update-slice), channel_id=1, replica_groups=mesh['dp'=8,'fsdp'=4] {'dp','fsdp'}, use_global_device_ids=true, to_apply=%add | all-reduce | flops 3072 | bytes 12288
  63.2 40.1 %all-gather = bf16[32,24,8]{1,2,0:T(8,128)(2,1)S(1)} all-gather(bf16[1,24,8]{1,2,0:T(8,128)(2,1)S(1)} %get-tuple-element.275), channel_id=1, replica_groups=mesh['dp'=8,'fsdp'=4] {'dp','fsdp'}, dimensions={0}, use_global_device_ids=true | all-gather | bytes 12672 | tf_op jit(solution)/shard_map/all_gather | solution.py:158
  106.5 1.7 copy.121
  108.2 1.6 broadcast_compare_fusion.1
  109.8 4.6 convert_reduce_fusion.2
  114.5 6.4 fusion.81
  120.8 3.6 copy-done.16
  125.8 1.7 copy.118
  127.5 5.1 fusion.36
  133.9 2.3 copy.117
  136.2 2.3 copy.119
  138.5 14.9 %fusion.97 = (f32[12,512]{1,0:T(8,128)S(1)}, f32[12,512,1024]{2,1,0:T(8,128)}) fusion(pred[512,1024]{1,0:T(8,128)(4,1)} %get-tuple-element.277, bf16[512,12,64]{0,2,1:T(8,128)(2,1)} %bitcast.105, bf16[1024,12,64]{0,2,1:T(8,128)(2,1)S(1)} %bitcast.99), kind=kOutput, calls=%fused_computation.190 | convolution fusion | flops 830473216 | bytes 28073984 | tf_op jit(solution)/shard_map/while/body/eval_jaxpr/sub | solution.py:74
  153.4 14.5 %fusion.98 = (f32[12,512]{1,0:T(8,128)S(1)}, f32[12,512,1024]{2,1,0:T(8,128)}) fusion(pred[512,1024]{1,0:T(8,128)(4,1)} %get-tuple-element.276, bf16[512,12,64]{0,2,1:T(8,128)(2,1)} %bitcast.109, bf16[1024,12,64]{0,2,1:T(8,128)(2,1)S(1)} %bitcast.100), kind=kOutput, calls=%fused_computation.191 | convolution fusion | flops 830473216 | bytes 28073984 | tf_op jit(solution)/shard_map/while/body/eval_jaxpr/sub | solution.py:74
  167.8 1.7 copy.116
  169.6 12.3 %fusion.46 = bf16[12,64,512]{2,1,0:T(8,128)(2,1)} fusion(bf16[1024,12,64]{0,2,1:T(8,128)(2,1)S(1)} %bitcast.115, f32[12,512,1024]{2,1,0:T(8,128)} %get-tuple-element.292, f32[12,512]{1,0:T(8,128)S(1)} %get-tuple-element.291), kind=kOutput, calls=%fused_computation.84 | convolution fusion | flops 818282496 | bytes 27549696 | tf_op jit(solution)/shard_map/while/body/eval_jaxpr/hqk,khd->qhd/dot_general | solution.py:77
  181.9 11.5 %fusion.43 = bf16[12,64,512]{2,1,0:T(8,128)(2,1)} fusion(bf16[1024,12,64]{0,2,1:T(8,128)(2,1)S(1)} %bitcast.116, f32[12,512,1024]{2,1,0:T(8,128)} %get-tuple-element.294, f32[12,512]{1,0:T(8,128)S(1)} %get-tuple-element.293), kind=kOutput, calls=%fused_computation.83 | convolution fusion | flops 818282496 | bytes 27549696 | tf_op jit(solution)/shard_map/while/body/eval_jaxpr/hqk,khd->qhd/dot_general | solution.py:77
  193.4 3.4 fusion.99
  196.9 1.6 copy-done.4
  199.0 11.2 %fusion.84 = f32[1024,3072]{1,0:T(8,128)} fusion(bf16[768,3072]{1,0:T(8,128)(2,1)} %all-gather.10.cloned.1.call-done, f32[1024,768]{0,1:T(8,128)} %copy-done.4, f32[768]{0:T(1024)S(1)} %get-tuple-element.227, f32[768]{0:T(1024)S(1)} %get-tuple-element.225, f32[1024]{0:T(1024)S(1)} %fusion.67, f32[1024]{0:T(1024)S(1)} %broadcast_multiply_fusion), kind=kOutput, calls=%fused_computation.179 | convolution fusion | flops 4835770368 | bytes 20461568 | tf_op jit(solution)/shard_map/dot_general | solution.py:34
  210.2 52.7 %all-gather.12.cloned.1.call-done = bf16[3072,768]{1,0:T(8,128)(2,1)} async-done(((bf16[96,768]{1,0:T(8,128)(2,1)}), bf16[3072,768]{1,0:T(8,128)(2,1)}) %all-gather.12.cloned.1.call-update) | async-done | bytes 4718608 | tf_op jit(solution)/shard_map/all_gather | solution.py:157
  262.9 16.5 %convert_reduce_fusion = (f32[3072]{0:T(1024)}, bf16[1024,3072]{1,0:T(8,128)(2,1)S(1)}) fusion(f32[1024,3072]{1,0:T(8,128)} %fusion.84, f32[3072]{0:T(1024)S(1)} %convert_element_type.124, bf16[1024,768]{0,1:T(8,128)(2,1)S(1)} %copy-done.27, bf16[3072,768]{1,0:T(8,128)(2,1)} %all-gather.12.cloned.1.call-done), kind=kOutput, calls=%fused_computation.21 | convolution fusion | flops 4904186880 | bytes 25190400 | tf_op jit(solution)/shard_map/dot_general | solution.py:44
  279.4 7.3 fusion.101
  286.7 3.7 copy.123
  290.4 3.6 multiply_reduce_fusion.2
  298.9 2.8 fusion.51
  304.8 18.9 %multiply_reduce_fusion.1 = (f32[12,512]{1,0:T(8,128)S(1)}, f32[12,512,1024]{2,1,0:T(8,128)}) fusion(f32[12,512,1024]{2,1,0:T(8,128)} %get-tuple-element.294, f32[12,512]{1,0:T(8,128)S(1)} %get-tuple-element.293, bf16[512,12,64]{0,2,1:T(8,128)(2,1)S(1)} %bitcast.119, bf16[1024,12,64]{0,2,1:T(8,128)(2,1)S(1)} %bitcast.117), kind=kOutput, calls=%fused_computation.5 | convolution fusion | flops 824174592 | bytes 52740096 | tf_op jit(solution)/shard_map/while/body/eval_jaxpr/qhd,khd->hqk/dot_general | solution.py:101
  323.7 16.7 %multiply_convert_fusion.1 = bf16[12,512,1024]{2,1,0:T(8,128)(2,1)S(1)} fusion(f32[12,512,1024]{2,1,0:T(8,128)} %get-tuple-element.299, f32[12,512]{1,0:T(8,128)S(1)} %get-tuple-element.298, f32[12,512,1024]{2,1,0:T(8,128)} %get-tuple-element.294, f32[12,512]{1,0:T(8,128)S(1)} %get-tuple-element.293), kind=kLoop, calls=%fused_computation.4 | loop fusion | flops 25165824 | bytes 62963712 | tf_op jit(solution)/shard_map/while/body/eval_jaxpr/convert_element_type | solution.py:107
  340.3 6.3 fusion.49
  346.6 5.2 fusion.103
  351.8 11.5 %fusion.17 = f32[12,64,1024]{2,1,0:T(8,128)} fusion(bf16[512,12,64]{0,2,1:T(8,128)(2,1)S(1)} %bitcast.121, f32[12,512,1024]{2,1,0:T(8,128)} %get-tuple-element.292, f32[12,512]{1,0:T(8,128)S(1)} %get-tuple-element.291), kind=kOutput, calls=%fused_computation.31 | convolution fusion | flops 817889280 | bytes 29122560 | tf_op jit(solution)/shard_map/while/body/eval_jaxpr/hqk,qhd->khd/dot_general | solution.py:117
  363.3 18.9 %multiply_reduce_fusion = (f32[12,512]{1,0:T(8,128)S(1)}, f32[12,512,1024]{2,1,0:T(8,128)}) fusion(f32[12,512,1024]{2,1,0:T(8,128)} %get-tuple-element.292, f32[12,512]{1,0:T(8,128)S(1)} %get-tuple-element.291, bf16[512,12,64]{0,2,1:T(8,128)(2,1)S(1)} %bitcast.122, bf16[1024,12,64]{0,2,1:T(8,128)(2,1)S(1)} %bitcast.118), kind=kOutput, calls=%fused_computation.3 | convolution fusion | flops 824174592 | bytes 52740096 | tf_op jit(solution)/shard_map/while/body/eval_jaxpr/qhd,khd->hqk/dot_general | solution.py:101
  382.3 16.9 %multiply_convert_fusion = bf16[12,512,1024]{2,1,0:T(8,128)(2,1)S(1)} fusion(f32[12,512,1024]{2,1,0:T(8,128)} %get-tuple-element.301, f32[12,512]{1,0:T(8,128)S(1)} %get-tuple-element.300, f32[12,512,1024]{2,1,0:T(8,128)} %get-tuple-element.292, f32[12,512]{1,0:T(8,128)S(1)} %get-tuple-element.291), kind=kLoop, calls=%fused_computation.2 | loop fusion | flops 25165824 | bytes 62963712 | tf_op jit(solution)/shard_map/while/body/eval_jaxpr/convert_element_type | solution.py:107
  399.3 6.3 fusion.50
  405.5 4.7 multiply_convert_fusion.3
  410.5 11.8 %add_convert_fusion = bf16[12,64,1024]{2,1,0:T(8,128)(2,1)S(1)} fusion(f32[12,64,1024]{2,1,0:T(8,128)} %fusion.17, bf16[512,12,64]{0,2,1:T(8,128)(2,1)} %bitcast.120, f32[12,512,1024]{2,1,0:T(8,128)} %get-tuple-element.294, f32[12,512]{1,0:T(8,128)S(1)} %get-tuple-element.293), kind=kOutput, calls=%fused_computation.67 | convolution fusion | flops 819462144 | bytes 30695424 | tf_op jit(solution)/shard_map/while/body/eval_jaxpr/hqk,qhd->khd/dot_general | solution.py:117
  423.5 7.0 fusion.39
  431.2 14.2 %fusion.85 = f32[3072,768]{1,0:T(8,128)} fusion(bf16[1024,768]{0,1:T(8,128)(2,1)} %get-tuple-element.255, f32[1024,3072]{1,0:T(8,128)} %fusion.84, f32[3072]{0:T(1024)S(1)} %copy-done.62), kind=kOutput, calls=%fused_computation.180 | convolution fusion | flops 4863295488 | bytes 23605248 | tf_op jit(solution)/shard_map/dot_general | solution.py:38
  446.1 10.8 %fusion.83 = f32[768,3072]{1,0:T(8,128)} fusion(bf16[1024,3072]{1,0:T(8,128)(2,1)} %copy-done.78, f32[1024,768]{0,1:T(8,128)} %copy-done.4, f32[768]{0:T(1024)S(1)} %copy-done.40, f32[768]{0:T(1024)S(1)} %copy-done.36, f32[1024]{0:T(1024)S(1)} %copy-done.38, f32[1024]{0:T(1024)S(1)} %copy-done.34), kind=kOutput, calls=%fused_computation.178 | convolution fusion | flops 4835770368 | bytes 18888704 | tf_op jit(solution)/shard_map/dot_general | solution.py:38
  457.6 12.8 %fusion.102 = (bf16[1024,768]{0,1:T(8,128)(2,1)}, f32[1024,768]{0,1:T(8,128)}) fusion(f32[1024,768]{0,1:T(8,128)} %copy-done.4, f32[768]{0:T(1024)S(1)} %copy-done.69, bf16[3072,768]{1,0:T(8,128)(2,1)} %all-gather.12.cloned.1.call-done, f32[1024,3072]{1,0:T(8,128)} %fusion.84, f32[3072]{0:T(1024)S(1)} %copy-done.62), kind=kOutput, calls=%fused_computation.195 | convolution fusion | flops 4865654784 | bytes 25181184 | tf_op jit(solution)/shard_map/dot_general | solution.py:34
  470.4 2.6 copy.127
  473.1 1.7 convert_reduce_fusion.4
  474.8 8.6 fusion.100
  483.7 3.9 copy.124
  487.7 2.6 fusion.35
  492.7 3.5 add_add_fusion.2
  496.2 3.8 copy.128
  500.0 2.9 convolution_bitcast_fusion
  505.3 100.1 %reduce-scatter.6.cloned.1.call-done = f32[24,2304]{1,0:T(8,128)} async-done(((f32[768,2304]{1,0:T(8,128)}), f32[24,2304]{1,0:T(8,128)}) %reduce-scatter.6.cloned.1.call-update) | async-done | bytes 221200 | tf_op jit(solution)/shard_map/reduce_scatter | solution.py:281
  607.8 138.9 %reduce-scatter.12.cloned.1.call-done = f32[96,768]{1,0:T(8,128)} async-done(((f32[3072,768]{1,0:T(8,128)}), f32[96,768]{1,0:T(8,128)}) %reduce-scatter.12.cloned.1.call-update) | async-done | bytes 294928 | tf_op jit(solution)/shard_map/reduce_scatter | solution.py:232
  749.1 139.7 %reduce-scatter.10.cloned.1.call-done = f32[24,3072]{1,0:T(8,128)} async-done(((f32[768,3072]{1,0:T(8,128)}), f32[24,3072]{1,0:T(8,128)}) %reduce-scatter.10.cloned.1.call-update) | async-done | bytes 294928 | tf_op jit(solution)/shard_map/reduce_scatter | solution.py:231
  891.2 6.5 concatenate.24
  897.7 41.5 %all-reduce.3 = (f32[2304]{0:T(1024)S(1)}, f32[768,8]{0,1:T(8,128)S(1)}, f32[3072]{0:T(1024)S(1)}, f32[17]{0:T(128)S(1)}, f32[768]{0:T(1024)S(1)}, /*index=5*/f32[3072]{0:T(1024)S(1)}, f32[768]{0:T(1024)S(1)}) all-reduce(f32[2304]{0:T(1024)S(1)} %get-tuple-element.221, ...), channel_id=1, replica_groups=mesh['dp'=8,'fsdp'=4] {'dp','fsdp'}, use_global_device_ids=true, to_apply=%region_18.19 | all-reduce | flops 16145 | bytes 129160 | tf_op jit(solution)/shard_map/psum | solution.py:305
  950.0 1.7 multiply_reduce_fusion.9
  953.1 1.6 multiply_reduce_fusion.11
  956.0 1.7 multiply_reduce_fusion.6
  958.4 1.7 multiply_reduce_fusion.5
  960.8 39.3 %psum.47 = f32[]{:T(128)} all-reduce(f32[]{:T(128)S(6)} %add.297), channel_id=1, replica_groups=mesh['dp'=8,'fsdp'=4] {'dp','fsdp'}, use_global_device_ids=true, to_apply=%region_59.60 | all-reduce | flops 1 | bytes 8 | tf_op jit(solution)/shard_map/psum | solution.py:330
  1002.6 1.6 divide_subtract_fusion.3
  1004.3 1.9 divide_subtract_fusion.2
  1006.2 1.8 divide_subtract_fusion
  (240 shorter events, 41.4 us)
Async XLA Ops:
  7.2 102.6 %copy-start = (f32[1,24,768]{2,1,0:T(8,128)S(1)}, f32[1,24,768]{2,1,0:T(8,128)}, u32[]{:S(2)}) copy-start(f32[1,24,768]{2,1,0:T(8,128)} %param.23) | copy-start | bytes 221188
  7.2 97.1 %copy-start.22 = (bf16[1024,768]{1,0:T(8,128)(2,1)S(1)}, bf16[1024,768]{1,0:T(8,128)(2,1)}, u32[]{:S(2)}) copy-start(bf16[1024,768]{1,0:T(8,128)(2,1)} %param.20) | copy-start | bytes 4718596
  7.2 107.2 %all-gather.6.cloned.1.call-start = ((), (), s32[]{:S(2)}) async-start(), calls=%async_computation.4 | async-start | bytes 3649536 | tf_op jit(solution)/shard_map/all_gather | solution.py:154
  9.7 183.7 %all-gather.8.cloned.1.call-start = ((), (), s32[]{:S(2)}) async-start(), calls=%async_computation.5 | async-start | bytes 1216512 | tf_op jit(solution)/shard_map/all_gather | solution.py:155
  12.0 187.0 %all-gather.10.cloned.1.call-start = ((), (), s32[]{:S(2)}) async-start(), calls=%async_computation.6 | async-start | bytes 4866048 | tf_op jit(solution)/shard_map/all_gather | solution.py:156
  14.4 248.5 %all-gather.12.cloned.1.call-start = ((), (), s32[]{:S(2)}) async-start(), calls=%async_computation.7 | async-start | bytes 4866048 | tf_op jit(solution)/shard_map/all_gather | solution.py:157
  16.8 486.1 %reduce-scatter.8.cloned.1.call-start = ((), (), s32[]{:S(2)}) async-start(), calls=%async_computation.9 | async-start | bytes 2433024 | tf_op jit(solution)/shard_map/reduce_scatter | solution.py:282
  63.2 199.7 %copy-start.61 = (f32[3072]{0:T(1024)}, f32[3072]{0:T(1024)S(1)}, u32[]{:S(2)}) copy-start(f32[3072]{0:T(1024)S(1)} %convert_element_type.124) | copy-start | bytes 36868
  104.3 10.1 copy-start.45
  104.3 10.1 copy-start.70
  104.3 94.7 %copy-start.39 = (f32[768]{0:T(1024)}, f32[768]{0:T(1024)S(1)}, u32[]{:S(2)}) copy-start(f32[768]{0:T(1024)S(1)} %get-tuple-element.227) | copy-start | bytes 9220
  104.3 189.7 %copy-start.35 = (f32[768]{0:T(1024)}, f32[768]{0:T(1024)S(1)}, u32[]{:S(2)}) copy-start(f32[768]{0:T(1024)S(1)} %get-tuple-element.225) | copy-start | bytes 9220
  105.1 88.3 %copy-start.2 = (bf16[1024,768]{0,1:T(8,128)(2,1)}, bf16[1024,768]{0,1:T(8,128)(2,1)S(1)}, u32[]{:S(2)}) copy-start(bf16[1024,768]{0,1:T(8,128)(2,1)S(1)} %copy.113) | copy-start | bytes 4718596
  105.4 4.5 copy-start.68
  105.4 9.1 copy-start.43
  106.5 8.0 copy-start.51
  108.2 6.3 copy-start.12
  127.5 25.9 %copy-start.15 = (bf16[1024,768]{0,1:T(8,128)(2,1)}, bf16[1024,768]{0,1:T(8,128)(2,1)S(1)}, u32[]{:S(2)}) copy-start(bf16[1024,768]{0,1:T(8,128)(2,1)S(1)} %copy.118) | copy-start | bytes 4718596
  169.6 12.3 %copy-start.24 = (bf16[1024,768]{0,1:T(8,128)(2,1)}, bf16[1024,768]{0,1:T(8,128)(2,1)S(1)}, u32[]{:S(2)}) copy-start(bf16[1024,768]{0,1:T(8,128)(2,1)S(1)} %copy.116) | copy-start | bytes 4718596
  196.9 97.1 %copy-start.33 = (f32[1024]{0:T(1024)}, f32[1024]{0:T(1024)S(1)}, u32[]{:S(2)}) copy-start(f32[1024]{0:T(1024)S(1)} %broadcast_multiply_fusion) | copy-start | bytes 12292
  198.9 95.1 %copy-start.37 = (f32[1024]{0:T(1024)}, f32[1024]{0:T(1024)S(1)}, u32[]{:S(2)}) copy-start(f32[1024]{0:T(1024)S(1)} %fusion.67) | copy-start | bytes 12292
  199.0 63.9 %copy-start.27 = (bf16[1024,768]{0,1:T(8,128)(2,1)S(1)}, bf16[1024,768]{0,1:T(8,128)(2,1)}, u32[]{:S(2)}) copy-start(bf16[1024,768]{0,1:T(8,128)(2,1)} %get-tuple-element.255) | copy-start | bytes 4718596
  199.0 80.4 %slice-start = ((s8[4718592]{0:T(1024)(128)(4,1)}), s8[524288]{0:T(1024)(128)(4,1)S(1)}, s32[]{:S(2)}) async-start(s8[4718592]{0:T(1024)(128)(4,1)} %bitcast.107), calls=%async_computation.12 | async-start | bytes 1048576
  262.9 16.5 %slice-start.1 = ((s8[4718592]{0:T(1024)(128)(4,1)}), s8[4194304]{0:T(1024)(128)(4,1)S(1)}, s32[]{:S(2)}) async-start(s8[4718592]{0:T(1024)(128)(4,1)} %bitcast.107), calls=%async_computation.13 | async-start | bytes 8388608
  279.4 7.3 copy-start.78
  294.9 3.8 copy-start.9
  295.0 3.8 copy-start.53
  304.1 19.6 %copy-start.30 = (bf16[512,768]{0,1:T(8,128)(2,1)}, bf16[512,768]{0,1:T(8,128)(2,1)S(1)}, u32[]{:S(2)}) copy-start(bf16[512,768]{0,1:T(8,128)(2,1)S(1)} %get-tuple-element.262) | copy-start | bytes 2359300
  346.6 5.2 copy-start.31
  351.8 11.5 %copy-start.26 = (bf16[1024,768]{0,1:T(8,128)(2,1)S(1)}, bf16[1024,768]{0,1:T(8,128)(2,1)}, u32[]{:S(2)}) copy-start(bf16[1024,768]{0,1:T(8,128)(2,1)} %copy-done.24) | copy-start | bytes 4718596
  351.8 11.5 %copy-start.32 = (bf16[512,768]{0,1:T(8,128)(2,1)S(1)}, bf16[512,768]{0,1:T(8,128)(2,1)}, u32[]{:S(2)}) copy-start(bf16[512,768]{0,1:T(8,128)(2,1)} %get-tuple-element.263) | copy-start | bytes 2359300
  382.3 223.2 %reduce-scatter.6.cloned.1.call-start = ((), (), s32[]{:S(2)}) async-start(), calls=%async_computation.8 | async-start | bytes 7299072 | tf_op jit(solution)/shard_map/reduce_scatter | solution.py:281
  405.5 4.7 copy-start.18
  405.5 4.7 copy-start.19
  410.2 12.1 %copy-start.17 = (bf16[12,64,1024]{2,1,0:T(8,128)(2,1)}, bf16[12,64,1024]{2,1,0:T(8,128)(2,1)S(1)}, u32[]{:S(2)}) copy-start(bf16[12,64,1024]{2,1,0:T(8,128)(2,1)S(1)} %multiply_convert_fusion.3) | copy-start | bytes 4718596
  410.4 13.0 %copy-start.3 = (bf16[1024,768]{0,1:T(8,128)(2,1)S(1)}, bf16[1024,768]{0,1:T(8,128)(2,1)}, u32[]{:S(2)}) copy-start(bf16[1024,768]{0,1:T(8,128)(2,1)} %copy-done.2) | copy-start | bytes 4718596
  410.5 13.0 %copy-start.44 = (f32[1024]{0:T(1024)S(1)}, f32[1024]{0:T(1024)}, u32[]{:S(2)}) copy-start(f32[1024]{0:T(1024)} %copy-done.43) | copy-start | bytes 12292
  410.5 13.0 %copy-start.46 = (f32[768]{0:T(1024)S(1)}, f32[768]{0:T(1024)}, u32[]{:S(2)}) copy-start(f32[768]{0:T(1024)} %copy-done.45) | copy-start | bytes 9220
  410.5 13.0 %copy-start.52 = (f32[1024]{0:T(1024)S(1)}, f32[1024]{0:T(1024)}, u32[]{:S(2)}) copy-start(f32[1024]{0:T(1024)} %copy-done.51) | copy-start | bytes 12292
  410.5 13.0 %copy-start.71 = (f32[768]{0:T(1024)S(1)}, f32[768]{0:T(1024)}, u32[]{:S(2)}) copy-start(f32[768]{0:T(1024)} %copy-done.70) | copy-start | bytes 9220
  430.5 316.2 %reduce-scatter.12.cloned.1.call-start = ((), (), s32[]{:S(2)}) async-start(), calls=%async_computation.11 | async-start | bytes 9732096 | tf_op jit(solution)/shard_map/reduce_scatter | solution.py:232
  445.4 443.3 %reduce-scatter.10.cloned.1.call-start = ((), (), s32[]{:S(2)}) async-start(), calls=%async_computation.10 | async-start | bytes 9732096 | tf_op jit(solution)/shard_map/reduce_scatter | solution.py:231
  483.7 6.6 copy-start.49
  483.7 8.1 copy-start.14
  487.7 4.2 copy-start.10
  496.2 3.8 copy-start.20
  500.0 446.0 %copy-start.63 = (f32[2304]{0:T(1024)S(1)}, f32[2304]{0:T(1024)}, u32[]{:S(2)}) copy-start(f32[2304]{0:T(1024)} %param.31) | copy-start | bytes 27652
  500.0 502.0 %copy-start.58 = (f32[24,8]{0,1:T(8,128)S(1)}, f32[24,8]{0,1:T(8,128)}, u32[]{:S(2)}) copy-start(f32[24,8]{0,1:T(8,128)} %param.28) | copy-start | bytes 2308
  500.0 506.1 %copy-start.28 = (f32[96,768]{1,0:T(8,128)S(1)}, f32[96,768]{1,0:T(8,128)}, u32[]{:S(2)}) copy-start(f32[96,768]{1,0:T(8,128)} %param.27) | copy-start | bytes 884740
  500.0 508.9 %copy-start.1 = (f32[1,24,768]{2,1,0:T(8,128)S(1)}, f32[1,24,768]{2,1,0:T(8,128)}, u32[]{:S(2)}) copy-start(f32[1,24,768]{2,1,0:T(8,128)} %param.23) | copy-start | bytes 221188
  503.0 505.0 %copy-start.29 = (f32[24,3072]{1,0:T(8,128)S(1)}, f32[24,3072]{1,0:T(8,128)}, u32[]{:S(2)}) copy-start(f32[24,3072]{1,0:T(8,128)} %param.26) | copy-start | bytes 884740
  505.3 503.5 %copy-start.66 = (f32[24]{0:T(128)}, f32[24]{0:T(128)S(1)}, u32[]{:S(2)}) copy-start(f32[24]{0:T(128)S(1)} %get-tuple-element.251) | copy-start | bytes 292
  607.8 401.0 %copy-start.67 = (f32[24]{0:T(128)}, f32[24]{0:T(128)S(1)}, u32[]{:S(2)}) copy-start(f32[24]{0:T(128)S(1)} %get-tuple-element.253) | copy-start | bytes 292
  749.1 259.7 %copy-start.64 = (f32[96]{0:T(128)}, f32[96]{0:T(128)S(1)}, u32[]{:S(2)}) copy-start(f32[96]{0:T(128)S(1)} %get-tuple-element.247) | copy-start | bytes 1156
  888.8 119.2 %copy-start.21 = (f32[24,3072]{1,0:T(8,128)S(1)}, f32[24,3072]{1,0:T(8,128)}, u32[]{:S(2)}) copy-start(f32[24,3072]{1,0:T(8,128)} %reduce-scatter.10.cloned.1.call-done) | copy-start | bytes 884740
  891.2 117.6 %copy-start.65 = (f32[24]{0:T(128)}, f32[24]{0:T(128)S(1)}, u32[]{:S(2)}) copy-start(f32[24]{0:T(128)S(1)} %get-tuple-element.249) | copy-start | bytes 292
  946.0 62.9 %copy-start.42 = (f32[2304]{0:T(1024)}, f32[2304]{0:T(1024)S(1)}, u32[]{:S(2)}) copy-start(f32[2304]{0:T(1024)S(1)} %multiply_add_fusion.5) | copy-start | bytes 27652
  947.3 61.5 %copy-start.73 = (f32[96]{0:T(128)}, f32[96]{0:T(128)S(1)}, u32[]{:S(2)}) copy-start(f32[96]{0:T(128)S(1)} %get-tuple-element.241) | copy-start | bytes 1156
  947.3 61.5 %copy-start.74 = (f32[96]{0:T(128)}, f32[96]{0:T(128)S(1)}, u32[]{:S(2)}) copy-start(f32[96]{0:T(128)S(1)} %get-tuple-element.242) | copy-start | bytes 1156
  948.7 60.2 %copy-start.56 = (f32[24,8]{0,1:T(8,128)}, f32[24,8]{0,1:T(8,128)S(1)}, u32[]{:S(2)}) copy-start(f32[24,8]{0,1:T(8,128)S(1)} %get-tuple-element.244) | copy-start | bytes 2308
  948.7 60.2 %copy-start.57 = (f32[24,8]{0,1:T(8,128)}, f32[24,8]{0,1:T(8,128)S(1)}, u32[]{:S(2)}) copy-start(f32[24,8]{0,1:T(8,128)S(1)} %get-tuple-element.245) | copy-start | bytes 2308
  953.1 55.8 %copy-start.47 = (f32[768]{0:T(1024)}, f32[768]{0:T(1024)S(1)}, u32[]{:S(2)}) copy-start(f32[768]{0:T(1024)S(1)} %get-tuple-element.310) | copy-start | bytes 9220
  953.1 55.8 %copy-start.50 = (f32[768]{0:T(1024)}, f32[768]{0:T(1024)S(1)}, u32[]{:S(2)}) copy-start(f32[768]{0:T(1024)S(1)} %get-tuple-element.311) | copy-start | bytes 9220
  956.0 52.9 %copy-start.41 = (f32[3072]{0:T(1024)}, f32[3072]{0:T(1024)S(1)}, u32[]{:S(2)}) copy-start(f32[3072]{0:T(1024)S(1)} %multiply_add_fusion.4) | copy-start | bytes 36868
  (25 other events, 47.2 us)
Sparse Core Ops, SparseCore 0:
  11.5 63.1 all-gather.5
  78.2 52.8 all-gather.7
  134.5 62.5 all-gather.9
  200.4 62.4 all-gather.11
  382.4 97.7 reduce-scatter.7
  487.3 118.1 reduce-scatter.5
  611.9 134.7 reduce-scatter.11
  754.2 134.5 reduce-scatter.9
where the time goes:
time: 1030 us; the launch traced here: 1020 us
  waiting for transfers between devices  432 us (42%)
  matrix products  247 us (24%)
  blocking collectives  164 us (16%)
  other arithmetic  98.1 us (10%)
  local copies, waits for them, and re-layouts  50 us (5%)
  between operations  27.2 us (3%)
    reduce_scatter x1, waiting for transfers between devices, per_device(): lax.psum_scatter(grad_w_up, ('dp', 'fsdp'), scatter_dimension=0, tiled=True)  140 us
    reduce_scatter x1, waiting for transfers between devices, per_device(): lax.psum_scatter(grad_w_down, ('dp', 'fsdp'), scatter_dimension=0, tiled=...  139 us
    reduce_scatter x1, waiting for transfers between devices, per_device(): lax.psum_scatter(grad_w_qkv, ('dp', 'fsdp'), scatter_dimension=0, tiled=T...  100 us
    all_gather x1, waiting for transfers between devices, per_device(): lax.all_gather(low_down, ('dp', 'fsdp'), axis=0, tiled=True)  52.7 us
    unnamed x1, blocking collectives  42.6 us
    psum x1, blocking collectives, per_device(): lax.psum((col_parts[0], col_parts[1], col_parts[2], col_parts[3], local_t...  41.5 us
    all_gather x1, blocking collectives, per_device(): lax.all_gather(low_vec, ('dp', 'fsdp'), axis=0, tiled=True)  40.1 us
    psum x1, blocking collectives, per_device(): norm_total = lax.psum(local_norm, ('dp', 'fsdp'))  39.3 us
  transfers between devices with their start and end apart: 8, of which 4 were waited for; matrix products, arithmetic and copies ran while one was open for 23% of the time, Pallas kernels for 0%

commit v1 on v0

v1 whole, which is shorter than its diff:
```python
import functools

import jax
import jax.numpy as jnp
from jax import lax
from jax.experimental import pallas as pl
from jax.experimental.pallas import tpu as pltpu
from jax.sharding import PartitionSpec as P

D = 768
HEADS = 12
HEAD_DIM = 64
FF = 3072
SEQ = 1024
STEP = 10
REACH = 64
QUERIES = 64
WINDOW = 192
GROUP = 4
WIDE = GROUP * HEAD_DIM

norm_eps = 1e-06
square_eps = 1e-30
clip_limit = 1.0
step_rate = 0.5
scale_floor = 0.001
decay = 1.0 - STEP ** (-0.8)

f32 = jnp.float32
bf16 = jnp.bfloat16
MESH = pl.DeviceIdType.MESH
VMEM_LIMIT = 60 * 1024 * 1024


def dot_nn(left, right):
    return jnp.dot(left, right, preferred_element_type=f32)


def dot_tn(left, right):
    return lax.dot_general(left, right, (((0,), (0,)), ((), ())), preferred_element_type=f32)


def dot_nt(left, right):
    return lax.dot_general(left, right, (((1,), (1,)), ((), ())), preferred_element_type=f32)


def span(index, size):
    return pl.ds(pl.multiple_of(index * size, size), size)


def columns(ref, index, size):
    cut = ref[(slice(None),) * (len(ref.shape) - 1) + (span(index, size),)]
    return cut.reshape(-1, size)


def normalise(values):
    centre = jnp.mean(values, -1, keepdims=True)
    centred = values - centre
    scale = lax.rsqrt(jnp.mean(centred * centred, -1, keepdims=True) + norm_eps)
    return centred * scale, scale


def normalise_back(grad, gain, unit, scale):
    inner = grad * gain
    along = jnp.mean(inner * unit, -1, keepdims=True)
    return scale * (inner - jnp.mean(inner, -1, keepdims=True) - unit * along)


def caption_bounds(ends, bounds):
    shape = (SEQ // QUERIES, GROUP * QUERIES)
    places = lax.broadcasted_iota(jnp.int32, shape, 0) * QUERIES
    places = places + lax.rem(lax.broadcasted_iota(jnp.int32, shape, 1), QUERIES)
    first = jnp.zeros(shape, jnp.int32)
    last = jnp.full(shape, SEQ - 1, jnp.int32)
    for index in range(ends.shape[1]):
        end = ends[0, index]
        first = jnp.where(places > end, jnp.maximum(first, end + 1), first)
        last = jnp.where(places <= end, jnp.minimum(last, end), last)
    bounds[0] = first
    bounds[1] = last


def tile_mask(bounds, tile, start):
    places = start + lax.broadcasted_iota(jnp.int32, (WINDOW, GROUP * QUERIES), 0)
    row = pl.ds(tile, 1)
    inside = (places >= bounds[0, row, :]) & (places <= bounds[1, row, :])
    return jnp.where(inside, 0.0, -1e30).astype(f32)


def window_start(tile):
    start = jnp.clip(tile * QUERIES - REACH, 0, SEQ - WINDOW)
    return pl.multiple_of(start, REACH)


def head_of(shape):
    return lax.broadcasted_iota(jnp.int32, shape, 1) // HEAD_DIM


def split_heads(rows):
    head, zero = head_of(rows.shape), jnp.zeros_like(rows)
    return jnp.concatenate([jnp.where(head == index, rows, zero) for index in range(GROUP)], 0)


def join_heads(blocks):
    shape = (blocks.shape[0] // GROUP, blocks.shape[1])
    head, result = head_of(shape), blocks[: shape[0]]
    for index in range(1, GROUP):
        result = jnp.where(head == index, blocks[index * shape[0] : (index + 1) * shape[0]], result)
    return result


def probabilities(keys, queries, mask):
    scores = dot_nt(keys, queries) + mask
    expo = jnp.exp(scores - jnp.max(scores, 0, keepdims=True))
    return expo * (1.0 / jnp.sum(expo, 0, keepdims=True))


def scaled(queries):
    return queries * jnp.asarray(HEAD_DIM ** (-0.5), queries.dtype)


def first_norm(tokens, vec, normed):
    def step(part, carry):
        rows = span(part, 256)
        unit, _ = normalise(tokens[rows, :].astype(f32))
        normed[rows, :] = (unit * vec[0:1, :] + vec[1:2, :]).astype(bf16)
        return carry

    lax.fori_loop(0, SEQ // 256, step, 0)


def project(normed, w_qkv, vec, proj):
    def step(part, carry):
        weight = columns(w_qkv, part, D)
        shift = jnp.where(part == 0, vec[4:5, :], jnp.where(part == 2, vec[5:6, :], 0.0))
        for half in range(2):
            rows = pl.ds(half * 512, 512)
            proj[rows, span(part, D)] = (dot_nn(normed[rows, :], weight) + shift).astype(bf16)
        return carry

    lax.fori_loop(0, 3, step, 0)


def attend_tile(tile, proj, bounds, mixed):
    start = window_start(tile)
    rows, window = span(tile, QUERIES), pl.ds(start, WINDOW)
    mask = tile_mask(bounds, tile, start)
    for at in range(0, D, WIDE):
        queries = split_heads(scaled(proj[rows, at : at + WIDE]))
        keys = proj[window, D + at : D + at + WIDE]
        values = proj[window, 2 * D + at : 2 * D + at + WIDE]
        probs = probabilities(keys, queries, mask).astype(bf16)
        mixed[rows, at : at + WIDE] = join_heads(dot_tn(probs, values)).astype(bf16)


def middle_part(part, tokens, mixed, w_out, vec, middle, normed):
    rows = span(part, 512)
    weight = w_out[...].reshape(D, D)
    value = tokens[rows, :].astype(f32) + (dot_nn(mixed[rows, :], weight) + vec[6:7, :])
    middle[rows, :] = value
    unit, _ = normalise(value)
    normed[rows, :] = (unit * vec[2:3, :] + vec[3:4, :]).astype(bf16)


def forward_kernel(tokens, ends, w_qkv, w_out, vec, normed, proj, mixed, middle, normed_two, bounds):
    first_norm(tokens, vec, normed)
    project(normed, w_qkv, vec, proj)
    caption_bounds(ends, bounds)

    def tile(index, carry):
        attend_tile(2 * index, proj, bounds, mixed)
        attend_tile(2 * index + 1, proj, bounds, mixed)
        return carry

    lax.fori_loop(0, SEQ // QUERIES // 2, tile, 0)

    def part(index, carry):
        middle_part(index, tokens, mixed, w_out, vec, middle, normed_two)
        return carry

    lax.fori_loop(0, SEQ // 512, part, 0)


def vmem(count):
    return [pl.BlockSpec(memory_space=pltpu.VMEM)] * count


SMEM = pl.BlockSpec(memory_space=pltpu.SMEM)


def forward_call(tokens, ends, w_qkv, w_out, vec):
    shape = jax.ShapeDtypeStruct
    return pl.pallas_call(
        forward_kernel,
        out_shape=(
            shape((SEQ, D), bf16),
            shape((SEQ, 3 * D), bf16),
            shape((SEQ, D), bf16),
            shape((SEQ, D), f32),
            shape((SEQ, D), bf16),
        ),
        in_specs=vmem(1) + [SMEM] + vmem(3),
        out_specs=tuple(vmem(5)),
        scratch_shapes=[pltpu.VMEM((2, SEQ // QUERIES, GROUP * QUERIES), jnp.int32)],
        compiler_params=pltpu.CompilerParams(vmem_limit_bytes=VMEM_LIMIT),
        name="forward",
    )(tokens, ends, w_qkv, w_out, vec)


def feed_kernel(
    normed,
    middle,
    w_up,
    w_down,
    vec,
    bias,
    cot_out,
    cot_pooled,
    ends,
    out,
    pooled,
    grad_middle,
    grad_up,
    grad_down,
    grad_small,
    final,
    grad_final,
    low_final,
    grad_normed,
    normed_t,
    hidden,
    grad_pre,
):
    wide, tall = D, 512
    grad_final[...] = cot_out[...].astype(f32)
    for index in range(ends.shape[1]):
        row = pl.ds(ends[0, index], 1)
        grad_final[row, :] = grad_final[row, :] + cot_pooled[0, index : index + 1, :]
    low_final[...] = grad_final[...].astype(bf16)
    grad_small[...] = jnp.zeros_like(grad_small)
    grad_small[7:8, :] = jnp.sum(low_final[...].astype(f32), 0, keepdims=True)
    final[...] = middle[...] + vec[7:8, :]
    grad_normed[...] = jnp.zeros_like(grad_normed)
    normed_t[...] = normed[...].T
    root = 0.7978845608028654
    cube = 0.044715

    def chunk(part, carry):
        place = span(part, wide)
        shift = bias[:, place]

        def rows_step(block, total):
            rows = span(block, tall)
            pre = dot_nn(normed[rows, :], w_up[:, place]) + shift
            square = pre * pre
            bend = jnp.tanh(root * (pre + cube * (square * pre)))
            half = 0.5 * (1.0 + bend)
            slope = half + 0.5 * pre * (1.0 - bend * bend) * (root + (3.0 * root * cube) * square)
            act = (pre * half).astype(bf16)
            hidden[rows, :] = act
            final[rows, :] = final[rows, :] + dot_nn(act, w_down[place, :])
            back = (dot_nt(low_final[rows, :], w_down[place, :]) * slope).astype(bf16)
            grad_pre[rows, :] = back
            grad_normed[rows, :] = grad_normed[rows, :] + dot_nt(back, w_up[:, place])
            return total + jnp.sum(back.astype(f32), 0, keepdims=True)

        total = lax.fori_loop(0, SEQ // tall, rows_step, jnp.zeros((1, wide), f32))
        grad_small[pl.ds(8 + part, 1), :] = total
        grad_down[place, :] = dot_tn(hidden[...], low_final[...]).astype(bf16)
        grad_up[:, place] = dot_nn(normed_t[...], grad_pre[...]).astype(bf16)
        return carry

    lax.fori_loop(0, FF // wide, chunk, 0)
    out[...] = final[...].astype(bf16)
    for index in range(ends.shape[1]):
        pooled[0, index : index + 1, :] = final[pl.ds(ends[0, index], 1), :]

    def back(part, carry):
        gain, shift = carry
        rows = span(part, 256)
        unit, scale = normalise(middle[rows, :])
        grad = grad_normed[rows, :]
        grad_middle[rows, :] = grad_final[rows, :] + normalise_back(grad, vec[2:3, :], unit, scale)
        return gain + jnp.sum(grad * unit, 0, keepdims=True), shift + jnp.sum(grad, 0, keepdims=True)

    zero = jnp.zeros((1, D), f32)
    gain, shift = lax.fori_loop(0, SEQ // 256, back, (zero, zero))
    grad_small[2:3, :] = gain
    grad_small[3:4, :] = shift


def feed_call(normed, middle, w_up, w_down, vec, bias, cot_out, cot_pooled, ends):
    shape = jax.ShapeDtypeStruct
    count = ends.shape[1]
    return pl.pallas_call(
        feed_kernel,
        out_shape=(
            shape((SEQ, D), bf16),
            shape((1, count, D), f32),
            shape((SEQ, D), f32),
            shape((D, FF), bf16),
            shape((FF, D), bf16),
            shape((16, D), f32),
        ),
        in_specs=vmem(8) + [SMEM],
        out_specs=tuple(vmem(6)),
        scratch_shapes=[
            pltpu.VMEM((SEQ, D), f32),
            pltpu.VMEM((SEQ, D), f32),
            pltpu.VMEM((SEQ, D), bf16),
            pltpu.VMEM((SEQ, D), f32),
            pltpu.VMEM((D, SEQ), bf16),
            pltpu.VMEM((SEQ, D), bf16),
            pltpu.VMEM((SEQ, D), bf16),
        ],
        compiler_params=pltpu.CompilerParams(vmem_limit_bytes=VMEM_LIMIT),
        name="feed_forward",
    )(normed, middle, w_up, w_down, vec, bias, cot_out, cot_pooled, ends)


def attend_tile_back(tile, proj, bounds, grad_mixed, grad_proj, grad_keys, grad_values):
    start = window_start(tile)
    rows, window = span(tile, QUERIES), pl.ds(start, WINDOW)
    mask = tile_mask(bounds, tile, start)
    for at in range(0, D, WIDE):
        here = slice(at, at + WIDE)
        queries = split_heads(scaled(proj[rows, here]))
        grads = split_heads(grad_mixed[rows, here])
        keys = proj[window, D + at : D + at + WIDE]
        values = proj[window, 2 * D + at : 2 * D + at + WIDE]
        probs = probabilities(keys, queries, mask)
        grad_probs = dot_nt(values, grads)
        along = jnp.sum(probs * grad_probs, 0, keepdims=True)
        grad_scores = (probs * (grad_probs - along)).astype(bf16)
        both = join_heads(dot_tn(grad_scores, keys)) * HEAD_DIM ** (-0.5)
        grad_proj[rows, here] = both.astype(bf16)
        grad_keys[window, here] += dot_nn(grad_scores, queries)
        grad_values[window, here] += dot_nn(probs.astype(bf16), grads)


def out_back_part(part, grad_middle, w_out, low_middle, grad_mixed, total):
    rows = span(part, 512)
    low = grad_middle[rows, :].astype(bf16)
    low_middle[rows, :] = low
    grad_mixed[rows, :] = dot_nt(low, w_out[...].reshape(D, D)).astype(bf16)
    return total + jnp.sum(low.astype(f32), 0, keepdims=True)


def finish_proj(grad_proj, grad_keys, grad_values, grad_small):
    grad_proj[:, D : 2 * D] = grad_keys[...].astype(bf16)
    grad_proj[:, 2 * D :] = grad_values[...].astype(bf16)
    grad_small[4:5, :] = jnp.sum(grad_proj[:, :D].astype(f32), 0, keepdims=True)
    grad_small[5:6, :] = jnp.sum(grad_proj[:, 2 * D :].astype(f32), 0, keepdims=True)


def project_back(normed_t, grad_proj, grad_qkv):
    def step(part, carry):
        place = span(part, D)
        grad_qkv[:, place] = dot_nn(normed_t[...], grad_proj[:, place]).astype(bf16)
        return carry

    lax.fori_loop(0, 3, step, 0)


def tokens_back(tokens, grad_proj, w_qkv, vec, grad_middle, grad_tokens, grad_small):
    def step(part, carry):
        gain, shift = carry
        rows = span(part, 512)
        grad = dot_nt(grad_proj[rows, :], w_qkv[...].reshape(D, 3 * D))
        unit, scale = normalise(tokens[rows, :].astype(f32))
        grad_tokens[rows, :] = grad_middle[rows, :] + normalise_back(grad, vec[0:1, :], unit, scale)
        return gain + jnp.sum(grad * unit, 0, keepdims=True), shift + jnp.sum(grad, 0, keepdims=True)

    zero = jnp.zeros((1, D), f32)
    gain, shift = lax.fori_loop(0, SEQ // 512, step, (zero, zero))
    grad_small[0:1, :] = gain
    grad_small[1:2, :] = shift


def backward_kernel(
    tokens,
    ends,
    w_qkv,
    w_out,
    vec,
    normed,
    proj,
    mixed,
    grad_middle,
    small,
    grad_tokens,
    grad_qkv,
    grad_out,
    grad_small,
    bounds,
    low_middle,
    grad_mixed,
    turned,
    grad_proj,
    grad_keys,
    grad_values,
):
    grad_small[...] = small[...]

    def part(index, total):
        return out_back_part(index, grad_middle, w_out, low_middle, grad_mixed, total)

    grad_small[6:7, :] = lax.fori_loop(0, SEQ // 512, part, jnp.zeros((1, D), f32))
    turned[...] = mixed[...].T
    grad_out[...] = dot_nn(turned[...], low_middle[...]).astype(bf16)
    caption_bounds(ends, bounds)
    grad_keys[...] = jnp.zeros_like(grad_keys)
    grad_values[...] = jnp.zeros_like(grad_values)

    def tile(index, carry):
        attend_tile_back(2 * index, proj, bounds, grad_mixed, grad_proj, grad_keys, grad_values)
        attend_tile_back(2 * index + 1, proj, bounds, grad_mixed, grad_proj, grad_keys, grad_values)
        return carry

    lax.fori_loop(0, SEQ // QUERIES // 2, tile, 0)
    finish_proj(grad_proj, grad_keys, grad_values, grad_small)
    turned[...] = normed[...].T
    project_back(turned, grad_proj, grad_qkv)
    tokens_back(tokens, grad_proj, w_qkv, vec, grad_middle, grad_tokens, grad_small)


def backward_call(tokens, ends, w_qkv, w_out, vec, normed, proj, mixed, grad_middle, small):
    shape = jax.ShapeDtypeStruct
    return pl.pallas_call(
        backward_kernel,
        out_shape=(
            shape((SEQ, D), f32),
            shape((D, 3 * D), bf16),
            shape((D, D), bf16),
            shape((16, D), f32),
        ),
        in_specs=vmem(1) + [SMEM] + vmem(8),
        out_specs=tuple(vmem(4)),
        scratch_shapes=[
            pltpu.VMEM((2, SEQ // QUERIES, GROUP * QUERIES), jnp.int32),
            pltpu.VMEM((SEQ, D), bf16),
            pltpu.VMEM((SEQ, D), bf16),
            pltpu.VMEM((D, SEQ), bf16),
            pltpu.VMEM((SEQ, 3 * D), bf16),
            pltpu.VMEM((SEQ, D), f32),
            pltpu.VMEM((SEQ, D), f32),
        ],
        compiler_params=pltpu.CompilerParams(vmem_limit_bytes=VMEM_LIMIT),
        name="backward",
    )(tokens, ends, w_qkv, w_out, vec, normed, proj, mixed, grad_middle, small)


class Place:
    def __init__(self, mesh_shape):
        line, face = mesh_shape["dp"] // 2, lax.axis_index("dp")
        cell = lax.axis_index("fsdp")
        self.line = line
        self.z, self.y = lax.div(face, 2), lax.rem(face, 2)
        self.x, self.c = lax.div(cell, 2), lax.rem(cell, 2)
        self.flat = face * 4 + cell
        self.fill()

    def fill(self):
        y, x, c = self.y, self.x, self.c
        self.near = (y + (1 - c) * (1 - 2 * y), x + c * (1 - 2 * x))
        self.far = (y + c * (1 - 2 * y), x + (1 - c) * (1 - 2 * x))
        self.cross = (1 - y, 1 - x)
        self.own = (y, x)

    def other(self):
        place = object.__new__(Place)
        place.line, place.z, place.y, place.x, place.c = self.line, self.z, self.y, self.x, 1 - self.c
        place.fill()
        return place

    def device(self, z, spot, c):
        return (z * 2 + spot[0], spot[1] * 2 + c)

    def sibling(self):
        return self.device(self.z, self.own, 1 - self.c)

    def along(self, step):
        return lax.rem(self.z + step, self.line)

    def peers(self):
        return [
            self.sibling(),
            self.device(self.z, self.near, self.c),
            self.device(self.z, self.far, self.c),
        ] + [self.device(self.along(step), self.own, self.c) for step in range(1, self.line)]


def greet(place):
    barrier = pltpu.get_barrier_semaphore()
    peers = place.peers()
    for peer in peers:
        pl.semaphore_signal(barrier, inc=1, device_id=peer, device_id_type=MESH)
    pl.semaphore_wait(barrier, len(peers))


def remote(source, target, send, recv, device):
    return pltpu.make_async_remote_copy(
        src_ref=source,
        dst_ref=target,
        send_sem=send,
        recv_sem=recv,
        device_id=device,
        device_id_type=MESH,
    )


def band(c, half):
    return pl.ds(pl.multiple_of(c * half, 128), half)


GATHER_SEMS = 20


class Gather:
    def __init__(self, place, shard, stage, whole, send, recv):
        self.place, self.shard, self.stage, self.whole = place, shard, stage, whole
        self.send, self.recv = send, recv
        self.rows, self.half = shard.shape[0], shard.shape[1] // 2

    def block(self, z, spot, c):
        return self.whole.at[z, spot[0], span(spot[1], 2 * self.rows), band(c, self.half)]

    def line(self, spot, c):
        return self.whole.at[:, spot[0], span(spot[1], 2 * self.rows), band(c, self.half)]

    def copy(self, ref, index, device, target=None):
        return remote(ref, ref if target is None else target, self.send.at[index], self.recv.at[index], device)

    def get(self, ref, index):
        self.copy(ref, index, self.place.sibling()).wait_recv()

    def swap_copy(self):
        p = self.place
        source = self.shard.at[:, band(1 - p.c, self.half)]
        return self.copy(source, 0, p.sibling(), self.stage.at[span(p.c, self.rows), :])

    def own_copies(self):
        p = self.place
        block = self.block(p.z, p.own, p.c)
        return [self.copy(block, step, p.device(p.along(step), p.own, p.c)) for step in range(1, p.line)]

    def on_copies(self):
        p = self.place
        ref = self.line(p.own, p.c)
        return [
            self.copy(ref, p.line, p.device(p.z, p.near, p.c)),
            self.copy(ref, p.line + 1, p.device(p.z, p.far, p.c)),
        ]

    def cross_copy(self):
        p = self.place
        return self.copy(self.line(p.near, p.c), p.line + 2, p.device(p.z, p.far, p.c))

    def hand_copy(self, group):
        p = self.place
        spot = (p.own, p.near, p.far, p.cross)[group]
        return self.copy(self.line(spot, p.c), p.line + 3 + group, p.sibling())

    def swap(self):
        p = self.place
        self.swap_copy().start()
        self.stage[span(p.c, self.rows), :] = self.shard[:, band(p.c, self.half)]

    def own(self):
        p = self.place
        self.get(self.stage.at[span(1 - p.c, self.rows), :], 0)
        self.whole[p.z, p.y, span(p.x, 2 * self.rows), band(p.c, self.half)] = self.stage[...].astype(bf16)
        for copy in self.own_copies():
            copy.start()

    def along_z(self):
        p = self.place
        for step in range(1, p.line):
            self.get(self.block(p.along(p.line - step), p.own, p.c), step)
        for copy in self.on_copies():
            copy.start()
        self.hand_copy(0).start()

    def from_near(self):
        p = self.place
        self.get(self.line(p.near, p.c), p.line)
        self.cross_copy().start()
        self.hand_copy(1).start()

    def from_far(self):
        p = self.place
        self.get(self.line(p.far, p.c), p.line + 1)
        self.hand_copy(2).start()
        self.get(self.line(p.cross, p.c), p.line + 2)
        self.hand_copy(3).start()

    def finish(self):
        o = self.place.other()
        for group, spot in enumerate((o.own, o.near, o.far, o.cross)):
            self.get(self.line(spot, o.c), o.line + 3 + group)

    def drain(self):
        self.swap_copy().wait_send()
        for copy in self.own_copies() + self.on_copies():
            copy.wait_send()
        self.cross_copy().wait_send()
        for group in range(4):
            self.hand_copy(group).wait_send()


class GatherPlanes(Gather):
    def pair(self, pair, spot, c):
        return self.whole.at[2 * pair : 2 * pair + 2, spot[0], span(spot[1], 2 * self.rows), band(c, self.half)]

    def on_copies(self, pair):
        p = self.place
        ref, index = self.pair(pair, p.own, p.c), p.line + 4 * pair
        return [
            self.copy(ref, index, p.device(p.z, p.near, p.c)),
            self.copy(ref, index + 1, p.device(p.z, p.far, p.c)),
        ]

    def cross_copy(self, pair):
        p = self.place
        return self.copy(self.pair(pair, p.near, p.c), p.line + 4 * pair + 2, p.device(p.z, p.far, p.c))

    def hand_copy(self, pair):
        p = self.place
        ref = self.whole.at[2 * pair : 2 * pair + 2, :, :, band(p.c, self.half)]
        return self.copy(ref, p.line + 4 * pair + 3, p.sibling())

    def along_z(self, pair):
        p = self.place
        for plane in (2 * pair, 2 * pair + 1):
            step = lax.rem(p.z - plane + p.line, p.line)

            @pl.when(step != 0)
            def _():
                self.get(self.block(plane, p.own, p.c), step)

        for copy in self.on_copies(pair):
            copy.start()

    def from_near(self, pair):
        p = self.place
        self.get(self.pair(pair, p.near, p.c), p.line + 4 * pair)
        self.cross_copy(pair).start()

    def from_far(self, pair):
        p = self.place
        self.get(self.pair(pair, p.far, p.c), p.line + 4 * pair + 1)
        self.get(self.pair(pair, p.cross, p.c), p.line + 4 * pair + 2)
        self.hand_copy(pair).start()

    def finish(self, pair):
        ref = self.whole.at[2 * pair : 2 * pair + 2, :, :, band(1 - self.place.c, self.half)]
        self.get(ref, self.place.line + 4 * pair + 3)

    def drain(self):
        self.swap_copy().wait_send()
        for copy in self.own_copies():
            copy.wait_send()
        for pair in range(self.place.line // 2):
            for copy in self.on_copies(pair):
                copy.wait_send()
            self.cross_copy(pair).wait_send()
            self.hand_copy(pair).wait_send()


class Spread:
    def __init__(self, place, tiles, send, recv):
        self.place, self.tiles, self.send, self.recv = place, tiles, send, recv

    def copy(self, ref, index, device):
        return remote(ref, ref, self.send.at[index], self.recv.at[index], device)

    def get(self, ref, index):
        self.copy(ref, index, self.place.sibling()).wait_recv()

    def chips(self, spot):
        return self.tiles.at[:, spot[0], spot[1]]

    def copies(self, stage):
        p = self.place
        far = p.device(p.z, p.far, p.c)
        if stage == 0:
            return [self.copy(self.tiles.at[p.z, p.y, p.x, p.c], 0, p.sibling())]
        if stage == 1:
            chip = self.tiles.at[p.z, p.y, p.x]
            return [self.copy(chip, step, p.device(p.along(step), p.own, p.c)) for step in range(1, p.line)]
        if stage == 2:
            return [
                self.copy(self.chips(p.own), p.line, p.device(p.z, p.near, p.c)),
                self.copy(self.chips(p.own), p.line + 1, far),
            ]
        return [self.copy(self.chips(p.near), p.line + 2, far)]

    def start(self, stage):
        for copy in self.copies(stage):
            copy.start()

    def first(self):
        self.start(0)

    def second(self):
        p = self.place
        self.get(self.tiles.at[p.z, p.y, p.x, 1 - p.c], 0)
        self.start(1)

    def third(self):
        p = self.place
        for step in range(1, p.line):
            self.get(self.tiles.at[p.along(p.line - step), p.y, p.x], step)
        self.start(2)

    def fourth(self):
        p = self.place
        self.get(self.chips(p.near), p.line)
        self.start(3)

    def finish(self):
        p = self.place
        self.get(self.chips(p.far), p.line + 1)
        self.get(self.chips(p.cross), p.line + 2)

    def drain(self):
        for stage in range(4):
            for copy in self.copies(stage):
                copy.wait_send()


def fill_tiles(place, tiles, olds, vectors, bias, moment_vec, moment_bias):
    here = (place.z, place.y, place.x, place.c)
    tiles[here] = jnp.zeros(tiles.shape[4:], tiles.dtype)
    tile = jnp.zeros(olds.shape[4:], f32)
    olds[here] = tile
    olds[here + (slice(0, 8), slice(0, vectors.shape[1]))] = vectors[...]
    olds[here + (slice(8, 9), slice(0, bias.shape[1]))] = bias[...]
    tiles[here] = olds[here].astype(tiles.dtype)
    olds[here] = tile
    olds[here + (slice(0, 8), slice(0, vectors.shape[1]))] = moment_vec[...]
    olds[here + (slice(8, 9), slice(0, bias.shape[1]))] = moment_bias[...]


def lay_out(tiles, first, size, out):
    lane = lax.broadcasted_iota(jnp.int32, (8, 128), 1)
    done = [jnp.zeros((8, 128), f32) for _ in range(out.shape[1] // 128)]
    line, count = tiles.shape[0], tiles.shape[0] * 8
    for index in range(count):
        tile = tiles[index // 8, index // 4 % 2, index // 2 % 2, index % 2].astype(f32)[first : first + 8]
        at, shift = divmod(index * size, 128)
        turned = pltpu.roll(tile, shift, 1) if shift else tile
        done[at] = jnp.where((lane >= shift) & (lane < shift + size), turned, done[at])
        if shift + size > 128:
            done[at + 1] = jnp.where(lane < shift + size - 128, turned, done[at + 1])
    for index, tile in enumerate(done):
        out[:, index * 128 : index * 128 + 128] = tile[: out.shape[0]]


class Reduce:
    def __init__(self, place, terms, other, far, got_far, near, got_near, line, got_line, whole, result, send, recv, mine=None):
        self.place, self.terms, self.other, self.mine = place, terms, other, mine
        self.far, self.got_far, self.near, self.got_near = far, got_far, near, got_near
        self.line, self.got_line, self.whole, self.result = line, got_line, whole, result
        self.send, self.recv = send, recv
        self.half = other.shape[-1]
        self.rows = whole.shape[0] // 2

    def copy(self, source, target, index, device):
        return remote(source, target, self.send.at[index], self.recv.at[index], device)

    def get(self, ref, index):
        self.copy(ref, ref, index, self.place.sibling()).wait_recv()

    def swap_copy(self):
        p = self.place
        return self.copy(self.terms.at[:, :, :, band(1 - p.c, self.half)], self.other, 0, p.sibling())

    def far_copy(self, group):
        p = self.place
        return self.copy(self.far.at[group], self.got_far.at[group], 1 + group, p.device(p.z, p.far, p.c))

    def near_copy(self):
        p = self.place
        return self.copy(self.near, self.got_near, 3, p.device(p.z, p.near, p.c))

    def line_copy(self, step):
        p = self.place
        target = p.device(p.along(step), p.own, p.c)
        return self.copy(self.line.at[step - 1], self.got_line.at[step - 1], 3 + step, target)

    def owner_copy(self):
        p = self.place
        source = self.whole.at[span(1 - p.c, self.rows), :]
        return self.copy(source, self.result.at[:, band(p.c, self.half)], 3 + p.line, p.sibling())

    def mine_copy(self):
        p = self.place
        source = self.terms.at[:, :, :, band(p.c, self.half)]
        return pltpu.make_async_copy(source, self.mine, self.send.at[4 + p.line])

    def swap(self):
        self.swap_copy().start()
        if self.mine is not None:
            self.mine_copy().start()

    def meet(self):
        self.get(self.other, 0)
        if self.mine is not None:
            self.mine_copy().wait()

    def pair(self, z, spot):
        rows = span(spot[1], 2 * self.rows)
        if self.mine is None:
            mine = self.terms[z, spot[0], rows, band(self.place.c, self.half)]
        else:
            mine = self.mine[z, spot[0], rows, :]
        return mine.astype(f32) + self.other[z, spot[0], rows, :].astype(f32)

    def to_far(self):
        p = self.place
        self.meet()
        for group, spot in enumerate((p.cross, p.far)):
            for z in range(p.line):
                self.far[group, z] = self.pair(z, spot).astype(bf16)
            self.far_copy(group).start()

    def to_near(self):
        p = self.place
        self.get(self.got_far.at[0], 1)
        for z in range(p.line):
            self.near[z] = (self.pair(z, p.near) + self.got_far[0, z].astype(f32)).astype(bf16)
        self.near_copy().start()

    def sum_own(self, z):
        return self.pair(z, self.place.own) + self.got_far[1, z].astype(f32) + self.got_near[z].astype(f32)

    def to_line(self):
        p = self.place
        self.get(self.got_far.at[1], 2)
        self.get(self.got_near, 3)
        self.send_line()

    def send_line(self):
        p = self.place
        for step in range(1, p.line):
            self.line[step - 1] = self.sum_own(p.along(step)).astype(bf16)
            self.line_copy(step).start()
        self.whole[...] = self.sum_own(p.z)

    def to_owner(self):
        p = self.place
        total = self.whole[...]
        for step in range(1, p.line):
            self.get(self.got_line.at[step - 1], 3 + step)
            total = total + self.got_line[step - 1].astype(f32)
        self.whole[...] = total
        self.owner_copy().start()
        self.result[:, band(p.c, self.half)] = self.whole[span(p.c, self.rows), :]

    def finish(self):
        p = self.place
        self.get(self.result.at[:, band(1 - p.c, self.half)], 3 + p.line)

    def drain(self):
        p = self.place
        self.swap_copy().wait_send()
        for group in range(2):
            self.far_copy(group).wait_send()
        self.near_copy().wait_send()
        for step in range(1, p.line):
            self.line_copy(step).wait_send()
        self.owner_copy().wait_send()


class ReducePlanes:
    def __init__(self, place, first, terms, other, far, got_far, near, got_near, line, got_line, whole, result, send, recv, mine=None):
        self.place, self.first, self.terms, self.other, self.mine = place, first, terms, other, mine
        self.far, self.got_far, self.near, self.got_near = far, got_far, near, got_near
        self.line, self.got_line, self.whole, self.result = line, got_line, whole, result
        self.send, self.recv = send, recv
        self.half = other.shape[-1]
        self.plane = first + place.c

    def copy(self, source, target, index, device):
        return remote(source, target, self.send.at[index], self.recv.at[index], device)

    def get(self, ref, index):
        self.copy(ref, ref, index, self.place.sibling()).wait_recv()

    def swap_copy(self):
        p = self.place
        return self.copy(self.terms.at[:, :, :, band(1 - p.c, self.half)], self.other, 0, p.sibling())

    def far_copy(self, group):
        p = self.place
        return self.copy(self.far.at[group], self.got_far.at[group], 1 + group, p.device(p.z, p.far, p.c))

    def near_copy(self):
        p = self.place
        return self.copy(self.near, self.got_near, 3, p.device(p.z, p.near, p.c))

    def line_copy(self):
        p = self.place
        step = lax.rem(self.plane - p.z + p.line, p.line)
        return self.copy(self.line, self.got_line.at[step - 1], 3 + step, p.device(self.plane, p.own, p.c))

    def owner_copy(self):
        p = self.place
        return self.copy(self.whole.at[1 - p.c], self.result, 3 + p.line, p.sibling())

    def mine_copy(self):
        p = self.place
        source = self.terms.at[:, :, :, band(p.c, self.half)]
        return pltpu.make_async_copy(source, self.mine, self.send.at[4 + p.line])

    def swap(self):
        self.swap_copy().start()
        if self.mine is not None:
            self.mine_copy().start()

    def meet(self):
        self.get(self.other, 0)
        if self.mine is not None:
            self.mine_copy().wait()

    def pair(self, spot):
        chip = spot[0] * 2 + spot[1]
        mine = self.terms[chip, :, :, band(self.place.c, self.half)] if self.mine is None else self.mine[chip]
        return mine.astype(f32) + self.other[chip].astype(f32)

    def to_far(self):
        p = self.place
        self.meet()
        for group, spot in enumerate((p.cross, p.far)):
            self.far[group] = self.pair(spot).astype(bf16)
            self.far_copy(group).start()

    def to_near(self):
        self.get(self.got_far.at[0], 1)
        self.near[...] = (self.pair(self.place.near) + self.got_far[0].astype(f32)).astype(bf16)
        self.near_copy().start()

    def to_line(self):
        p = self.place
        self.get(self.got_far.at[1], 2)
        self.get(self.got_near, 3)
        self.send_line(self.pair(p.own) + self.got_far[1].astype(f32) + self.got_near[...].astype(f32))

    def send_line(self, own):
        p = self.place

        @pl.when(p.z == self.plane)
        def _():
            self.whole[...] = own

        @pl.when(p.z != self.plane)
        def _():
            self.line[...] = own.astype(bf16)
            self.line_copy().start()

    def to_owner(self):
        p = self.place

        @pl.when(p.z == self.plane)
        def _():
            total = self.whole[...]
            for step in range(1, p.line):
                self.get(self.got_line.at[step - 1], 3 + step)
                total = total + self.got_line[step - 1].astype(f32)
            self.whole[...] = total
            self.owner_copy().start()
            self.result[...] = self.whole[p.c]

    def finish(self):
        p = self.place

        @pl.when(p.z == self.first + 1 - p.c)
        def _():
            self.get(self.result, 3 + p.line)

    def drain(self):
        p = self.place
        self.swap_copy().wait_send()
        for group in range(2):
            self.far_copy(group).wait_send()
        self.near_copy().wait_send()
        self.drain_line()

    def drain_line(self):
        p = self.place

        @pl.when(p.z == self.plane)
        def _():
            self.owner_copy().wait_send()

        @pl.when(p.z != self.plane)
        def _():
            self.line_copy().wait_send()


class ReduceStart(Reduce):
    def __init__(self, place, terms, other, far, got_far, near, own, send, recv):
        self.place, self.terms, self.other, self.mine = place, terms, other, None
        self.far, self.got_far, self.near, self.own = far, got_far, near, own
        self.send, self.recv = send, recv
        self.half = other.shape[-1]
        self.rows = own.shape[1] // 2

    def pass_sum(self):
        p = self.place
        self.get(self.got_far.at[0], 1)
        self.get(self.got_far.at[1], 2)
        for z in range(p.line):
            self.near[z] = (self.pair(z, p.near) + self.got_far[0, z].astype(f32)).astype(bf16)
            self.own[z] = self.pair(z, p.own) + self.got_far[1, z].astype(f32)

    def drain(self):
        self.swap_copy().wait_send()
        for group in range(2):
            self.far_copy(group).wait_send()


class ReducePlanesStart(ReducePlanes):
    def __init__(self, place, terms, other, far, got_far, near, own, send, recv):
        self.place, self.terms, self.other, self.mine = place, terms, other, None
        self.far, self.got_far, self.near, self.own = far, got_far, near, own
        self.send, self.recv = send, recv
        self.half = other.shape[-1]

    def pass_sum(self):
        p = self.place
        self.get(self.got_far.at[0], 1)
        self.get(self.got_far.at[1], 2)
        self.near[...] = (self.pair(p.near) + self.got_far[0].astype(f32)).astype(bf16)
        self.own[...] = self.pair(p.own) + self.got_far[1].astype(f32)

    def drain(self):
        self.swap_copy().wait_send()
        for group in range(2):
            self.far_copy(group).wait_send()


class ReduceRest(Reduce):
    def __init__(self, place, near, own, got_near, line, got_line, whole, result, send, recv):
        self.place, self.near, self.own, self.got_near = place, near, own, got_near
        self.line, self.got_line, self.whole, self.result = line, got_line, whole, result
        self.send, self.recv = send, recv
        self.half = near.shape[-1]
        self.rows = whole.shape[0] // 2

    def to_near(self):
        self.near_copy().start()

    def sum_own(self, z):
        return self.own[z] + self.got_near[z].astype(f32)

    def to_line(self):
        p = self.place
        self.get(self.got_near, 3)
        self.send_line()

    def drain(self):
        p = self.place
        self.near_copy().wait_send()
        for step in range(1, p.line):
            self.line_copy(step).wait_send()
        self.owner_copy().wait_send()


class ReducePlanesRest(ReducePlanes):
    def __init__(self, place, first, near, own, got_near, line, got_line, whole, result, send, recv):
        self.place, self.first, self.near, self.own, self.got_near = place, first, near, own, got_near
        self.line, self.got_line, self.whole, self.result = line, got_line, whole, result
        self.send, self.recv = send, recv
        self.half = near.shape[-1]
        self.plane = first + place.c

    def to_near(self):
        self.near_copy().start()

    def to_line(self):
        self.get(self.got_near, 3)
        self.send_line(self.own[...] + self.got_near[...].astype(f32))

    def drain(self):
        self.near_copy().wait_send()
        self.drain_line()


def reduce_scratch(line, rows, half, count):
    return [
        pltpu.VMEM((count, line, 2, 2 * rows, half), bf16),
        pltpu.VMEM((count, 2, line, rows, half), bf16),
        pltpu.VMEM((count, 2, line, rows, half), bf16),
        pltpu.VMEM((count, line, rows, half), bf16),
        pltpu.VMEM((count, line, rows, half), bf16),
        pltpu.VMEM((count, line - 1, rows, half), bf16),
        pltpu.VMEM((count, line - 1, rows, half), bf16),
        pltpu.VMEM((count, rows, half), f32),
    ]


def plane_scratch(line, rows, half, count):
    block = (2, rows, half)
    return [
        pltpu.VMEM((count, 4) + block, bf16),
        pltpu.VMEM((count, 2) + block, bf16),
        pltpu.VMEM((count, 2) + block, bf16),
        pltpu.VMEM((count,) + block, bf16),
        pltpu.VMEM((count,) + block, bf16),
        pltpu.VMEM((count,) + block, bf16),
        pltpu.VMEM((count, line - 1) + block, bf16),
        pltpu.VMEM((count,) + block, f32),
    ]


class AllSum:
    def __init__(self, place, value, slots, line, send, recv):
        self.place, self.value, self.slots, self.line = place, value, slots, line
        self.send, self.recv = send, recv

    def start(self, stage):
        p = self.place
        device = (p.sibling(), p.device(p.z, (p.y, 1 - p.x), p.c), p.device(p.z, (1 - p.y, p.x), p.c))[stage]
        self.copy = remote(self.value, self.slots.at[stage], self.send.at[stage], self.recv.at[stage], device)
        self.copy.start()

    def end(self, stage):
        self.copy.wait()
        self.value[...] = self.value[...] + self.slots[stage]

    def start_line(self):
        p = self.place
        self.line[p.z] = self.value[...]
        self.copies = [
            remote(self.line.at[p.z], self.line.at[p.z], self.send.at[2 + step], self.recv.at[2 + step],
                   p.device(p.along(step), p.own, p.c))
            for step in range(1, p.line)
        ]
        for copy in self.copies:
            copy.start()

    def end_line(self):
        p = self.place
        for step in range(1, p.line):
            ref = self.line.at[p.along(p.line - step)]
            remote(ref, ref, self.send.at[2 + step], self.recv.at[2 + step], p.sibling()).wait_recv()
        total = self.line[0]
        for z in range(1, p.line):
            total = total + self.line[z]
        self.value[...] = total
        for copy in self.copies:
            copy.wait_send()

    def next(self, stage):
        self.end(stage)
        if stage < 2:
            self.start(stage + 1)
        else:
            self.start_line()


def sum_scratch(line, rows):
    return [
        pltpu.VMEM((rows, D), f32),
        pltpu.VMEM((3, rows, D), f32),
        pltpu.VMEM((line, rows, D), f32),
        pltpu.SemaphoreType.DMA((2 + line,)),
        pltpu.SemaphoreType.DMA((2 + line,)),
    ]


def diagonal(size):
    return lax.broadcasted_iota(jnp.int32, (size, size), 0) == lax.broadcasted_iota(jnp.int32, (size, size), 1)


def to_column(row):
    return jnp.sum(jnp.where(diagonal(row.shape[1]), row, 0.0), 1, keepdims=True)


def to_row(column):
    return jnp.sum(jnp.where(diagonal(column.shape[0]), column, 0.0), 0, keepdims=True)


def total(values):
    return jnp.sum(jnp.sum(values, 1, keepdims=True), 0, keepdims=True)


def own_vectors(place, small, size):
    shape = (size, D)
    pick = lax.broadcasted_iota(jnp.int32, shape, 1) == place.flat * size + lax.broadcasted_iota(jnp.int32, shape, 0)
    row = lax.broadcasted_iota(jnp.int32, (8, size), 0)
    result = jnp.zeros((8, size), f32)
    for index in range(8):
        column = jnp.sum(jnp.where(pick, small[index : index + 1, :], 0.0), 1, keepdims=True)
        result = jnp.where(row == index, to_row(column), result)
    return result


def own_bias(place, small, size):
    per = D // size
    row, at = lax.div(place.flat, per), lax.rem(place.flat, per) * size
    shape = (FF // D, D)
    kept = lax.broadcasted_iota(jnp.int32, shape, 0) == row
    line = jnp.sum(jnp.where(kept, small[8 : 8 + FF // D, :], 0.0), 0, keepdims=True)
    shape = (size, D)
    pick = lax.broadcasted_iota(jnp.int32, shape, 1) == at + lax.broadcasted_iota(jnp.int32, shape, 0)
    return to_row(jnp.sum(jnp.where(pick, line, 0.0), 1, keepdims=True))


ROW_COUNTS = (D, D, D, FF)
SIZES = (3 * D * D, D * D, D * FF, FF * D)


def row_statistic(grad, old):
    mean = jnp.sum(grad * grad + square_eps, 1, keepdims=True) * (1.0 / grad.shape[1])
    return decay * to_column(old) + (1.0 - decay) * mean


def moment_of(grad, old):
    return decay * old + (1.0 - decay) * (grad * grad + square_eps)


def finish_kernel(*refs):
    refs = list(refs)

    def take(count):
        taken = refs[:count]
        del refs[:count]
        return taken

    large, grads, (grad_vec, grad_bias, stats), weights, (vectors, bias), rows, cols, (moment_vec, moment_bias) = (
        take(3), take(4), take(3), take(4), take(2), take(4), take(4), take(2)
    )
    out_large, out_grads, new_rows, new_cols, new_weights = take(3), take(4), take(4), take(4), take(4)
    out_vec, new_moment_vec, new_vec, out_bias, new_moment_bias, new_bias, clip_out = take(7)
    held, sems = take(3), take(1)[0]
    copies = []
    for index, count in enumerate((4, 1, 8)):
        size = held[index].shape[0] // count
        for part in range(count):
            piece, at = pl.ds(part * size, size), len(copies)
            copies.append(
                (
                    pltpu.make_async_copy(large[index].at[piece], held[index].at[piece], sems.at[0, at]),
                    pltpu.make_async_copy(held[index].at[piece], out_large[index].at[piece], sems.at[1, at]),
                )
            )
    for copy_in, _ in copies:
        copy_in.start()
    sums = stats[18:19, :]

    def one(index):
        return sums[:, index : index + 1]

    norm = one(17)
    at = 0
    col_rows, row_means = [], []
    for index in range(4):
        width = grads[index].shape[1]
        count = width // D
        sums_of = jnp.concatenate([stats[at + part : at + part + 1, :] for part in range(count)], 1)
        weighed = jnp.concatenate([stats[9 + at + part : 10 + at + part, :] for part in range(count)], 1)
        at += count
        col = decay * cols[index][...].reshape(1, width) + (1.0 - decay) * (sums_of * (1.0 / ROW_COUNTS[index]))
        new_cols[index][...] = col.reshape(width)
        col_rows.append(col)
        row_sum = decay * one(index) + (1.0 - decay) * (total(sums_of) * (1.0 / width))
        row_means.append(row_sum * (1.0 / ROW_COUNTS[index]))
        norm = norm + total(weighed / col) * row_means[index]
    for copy_in, copy_out in copies:
        copy_in.wait()
        copy_out.start()
    param_count = sum(SIZES) + 8 * D + FF
    clip = jnp.maximum(1.0, jnp.sqrt(norm * (1.0 / param_count)) * (1.0 / clip_limit))
    clip_out[...] = clip
    for index in range(4):
        grad = grads[index][...]
        out_grads[index][...] = grad
        row = row_statistic(grad, rows[index][...])
        new_rows[index][...] = to_row(row)
        scale = jnp.maximum(scale_floor, jnp.sqrt(one(4 + index) * (1.0 / SIZES[index])))
        update = grad * lax.rsqrt(row * col_rows[index] / row_means[index])
        new_weights[index][...] = weights[index][...] - (step_rate * scale / clip) * update
    lane = lax.broadcasted_iota(jnp.int32, (8, 1), 0)
    scale = jnp.zeros((8, 1), f32)
    for index in range(8):
        scale = jnp.where(lane == index, one(8 + index), scale)
    scale = jnp.maximum(scale_floor, jnp.sqrt(scale * (1.0 / D)))
    vec = grad_vec[...]
    moment = moment_of(vec, moment_vec[...])
    out_vec[...] = vec
    new_moment_vec[...] = moment
    new_vec[...] = vectors[...] - (step_rate * scale / clip) * (vec * lax.rsqrt(moment))
    scale = jnp.maximum(scale_floor, jnp.sqrt(one(16) * (1.0 / FF)))
    low = grad_bias[...]
    moment = moment_of(low, moment_bias[...])
    out_bias[...] = low
    new_moment_bias[...] = moment
    new_bias[...] = bias[...] - (step_rate * scale / clip) * (low * lax.rsqrt(moment))
    for _, copy_out in copies:
        copy_out.wait()


def finish_call(large, summed, weights, vectors, bias, rows, cols, moment_vec, moment_bias):
    shape = jax.ShapeDtypeStruct
    like = [shape(w.shape, f32) for w in weights]
    vec, low = shape(vectors.shape, f32), shape(bias.shape, f32)
    return pl.pallas_call(
        finish_kernel,
        out_shape=tuple(
            [shape(value.shape, value.dtype) for value in large]
            + like
            + [shape(r.shape, f32) for r in rows]
            + [shape(c.shape, f32) for c in cols]
            + like
            + [vec, vec, vec, low, low, low, shape((1, 1), f32)]
        ),
        in_specs=[pl.BlockSpec(memory_space=pl.ANY)] * 3 + vmem(23),
        out_specs=tuple([pl.BlockSpec(memory_space=pl.ANY)] * 3 + vmem(23)),
        scratch_shapes=[pltpu.VMEM(value.shape, value.dtype) for value in large] + [pltpu.SemaphoreType.DMA((2, 13))],
        compiler_params=pltpu.CompilerParams(vmem_limit_bytes=VMEM_LIMIT),
        name="finish",
    )(*large, *summed, *weights, vectors, bias, *rows, *cols, moment_vec, moment_bias)


def pooled_rows(ends, cot_pooled, parts):
    lane = lax.rem(lax.broadcasted_iota(jnp.int32, (1, 96), 1), 32)
    spot = jnp.full((1, 96), -1, jnp.int32)
    for index in range(ends.shape[1]):
        spot = jnp.where(lane == index, ends[0, index], spot)
    left = cot_pooled[0]
    parts[...] = jnp.zeros_like(parts)
    for index in range(3):
        low = left.astype(bf16)
        parts[32 * index : 32 * index + left.shape[0], :] = low
        left = left - low.astype(f32)
    return spot


def attend_group(tile, group, proj, masks, mixed):
    start = window_start(tile)
    rows, window, at = span(tile, QUERIES), pl.ds(start, WINDOW), group * D
    mask = masks[tile]
    queries = split_heads(scaled(proj[rows, at : at + WIDE]))
    keys = proj[window, at + WIDE : at + 2 * WIDE]
    values = proj[window, at + 2 * WIDE : at + D]
    probs = probabilities(keys, queries, mask).astype(bf16)
    return rows, join_heads(dot_tn(probs, values)).astype(bf16)


def feed_rows(rows, cols, normed, up, down, bias, low_final, hidden, grad_pre, final, grad_normed):
    root = 0.7978845608028654
    cube = 0.044715
    pre = dot_nn(normed[rows, :], up()) + bias[0:1, cols]
    square = pre * pre
    half = 0.5 + 0.5 * jnp.tanh(pre * (root + (root * cube) * square))
    act = pre * half
    slope = half + act * ((1.0 - half) * (2.0 * root + (6.0 * root * cube) * square))
    act = act.astype(bf16)
    hidden[rows, :] = act
    final[rows, :] = final[rows, :] + dot_nn(act, down())
    back = (dot_nt(low_final[rows, :], down()) * slope).astype(bf16)
    grad_pre[rows, :] = back
    grad_normed[rows, :] = grad_normed[rows, :] + dot_nt(back, up())
    return jnp.sum(back.astype(f32), 0, keepdims=True)


def front_kernel(mesh_shape, *refs):
    refs = list(refs)

    def take(count):
        taken = refs[:count]
        del refs[:count]
        return taken

    tokens, ends, cot_out, cot_pooled, w_qkv, w_out, w_up, w_down = take(8)
    vectors, bias, moment_vec, moment_bias = take(4)
    out_both, out_normed, out_proj, out_mixed, out_tokens, out_middle, out_up, out_down, out_masks = take(9)
    vec, moments, pooled, grad_small, near_up, own_up, near_down, own_down = take(8)
    shards, stage, stage_down, weights, all_down, tiles, olds, all_bias = take(8)
    normed, proj, mixed, middle, normed_two, final, grad_middle, grad_normed, normed_t = take(9)
    bounds, masks, parts = take(3)
    up_scratch, down_scratch = take(3), take(3)
    send, recv, sum_send, sum_recv, tile_send, tile_recv, old_send, old_recv, out_sems = take(9)

    place = Place(mesh_shape)
    line = place.line
    cut = (line, 2, D // (2 * line), D)
    copies = {}

    def leave(name, source, target):
        copies[name] = pltpu.make_async_copy(source, target, out_sems.at[len(copies)])
        copies[name].start()

    spread = Spread(place, tiles, tile_send, tile_recv)
    old_spread = Spread(place, olds, old_send, old_recv)

    def gather_of(index, first, last):
        whole, half = slice(first * D, last * D), slice(first * D // 2, last * D // 2)
        return Gather(
            place, shards.at[:, whole], stage.at[:, half], weights.at[:, :, :, whole], send.at[index], recv.at[index]
        )

    g0, g1, g2, u0, u1 = (gather_of(*given) for given in ((0, 0, 1), (1, 1, 2), (2, 2, 3), (3, 3, 6), (4, 6, 8)))
    down = GatherPlanes(place, w_down, stage_down, all_down, send.at[5], recv.at[5])

    def begin():
        fill_tiles(place, tiles, olds, vectors, bias, moment_vec, moment_bias)
        greet(place)

    def lay_qkv():
        for group in range(3):
            for part in range(3):
                at = group * D + part * WIDE
                shards[:, at : at + WIDE] = w_qkv[:, part * D + group * WIDE : part * D + (group + 1) * WIDE]

    def lay_rest():
        shards[:, 3 * D : 4 * D] = w_out[...]
        shards[:, 4 * D :] = w_up[...]

    def cotangent():
        spot = pooled_rows(ends, cot_pooled, parts)
        caption_bounds(ends, bounds)

        def mask_of(tile, carry):
            masks[tile] = tile_mask(bounds, tile, window_start(tile))
            return carry

        lax.fori_loop(0, SEQ // QUERIES, mask_of, 0)
        leave("masks", masks, out_masks)

        def rows_of(part, carry):
            rows = span(part, 256)
            place_of = part * 256 + lax.broadcasted_iota(jnp.int32, (256, 96), 0)
            picked = dot_nn(jnp.where(place_of == spot, 1.0, 0.0).astype(bf16), parts[...])
            grad_middle[rows, :] = cot_out[rows, :].astype(f32) + picked
            return carry

        lax.fori_loop(0, SEQ // 256, rows_of, 0)

    def norm_tokens():
        lay_out(tiles, 0, vectors.shape[1], vec)
        first_norm(tokens, vec, normed)
        leave("normed", normed, out_normed)

    def project_group(group):
        at = group * D
        here = slice(group * WIDE, (group + 1) * WIDE)
        shift = jnp.concatenate([vec[4:5, here], jnp.zeros((1, WIDE), f32), vec[5:6, here]], 1)

        def half(part, carry):
            rows = span(part, 512)
            weight = weights[:, :, :, at : at + D].reshape(D, D)
            proj[rows, at : at + D] = (dot_nn(normed[rows, :], weight) + shift).astype(bf16)
            return carry

        lax.fori_loop(0, SEQ // 512, half, 0)

    def attend(group, *calls):
        here = slice(group * WIDE, (group + 1) * WIDE)
        each = SEQ // QUERIES // 4

        def tile(index, carry):
            for inner in range(4):
                rows, value = attend_group(4 * index + inner, group, proj, masks, mixed)
                mixed[rows, here] = value

            @pl.when(index == each // 2 - 1)
            def _():
                for call in calls:
                    call()

            return carry

        lax.fori_loop(0, each, tile, 0)

    def middle_rows():
        leave("both", weights.at[:, :, :, 0 : 4 * D], out_both)
        leave("mixed", mixed, out_mixed)
        leave("proj", proj, out_proj)

        def part(index, carry):
            middle_part(index, tokens, mixed, weights.at[:, :, :, 3 * D : 4 * D], vec, middle, normed_two)
            return carry

        lax.fori_loop(0, SEQ // 512, part, 0)

    hidden, grad_pre, low_final = proj.at[:, 0:D], proj.at[:, D : 2 * D], proj.at[:, 2 * D :]

    def prepare():
        normed_t[...] = normed_two[...].T
        final[...] = middle[...] + vec[7:8, :]
        grad_normed[...] = jnp.zeros_like(grad_normed)
        grad_small[...] = jnp.zeros_like(grad_small)
        lay_out(tiles, 8, bias.shape[1], all_bias)
        for name in ("normed", "both", "mixed", "proj"):
            copies[name].wait()
        u0.drain()
        low_final[...] = grad_middle[...].astype(bf16)
        grad_small[7:8, :] = jnp.sum(low_final[...].astype(f32), 0, keepdims=True)

    up_sum = ReduceStart(place, weights.at[:, :, :, 0 : 2 * D], *up_scratch, near_up, own_up, sum_send.at[0], sum_recv.at[0])
    down_sum = ReducePlanesStart(
        place, weights.at[:, :, :, 2 * D : 4 * D], *down_scratch, near_down, own_down, sum_send.at[1], sum_recv.at[1]
    )

    def chunk_copies(chunk):
        which = chunk - 2
        return (
            pltpu.make_async_copy(
                weights.at[:, :, :, span(2 * chunk, D)], out_up.at[:, :, :, span(which, D)], out_sems.at[10 + which]
            ),
            pltpu.make_async_copy(
                weights.at[:, :, :, span(2 * chunk + 1, D)], out_down.at[:, :, :, span(which, D)], out_sems.at[12 + which]
            ),
        )

    def feed(chunk, carry):
        later = chunk // 2

        def when(value, *calls):
            @pl.when(chunk == value)
            def _():
                for call in calls:
                    call()

        def up_weight():
            return columns(weights, 4 + chunk, D)

        def down_weight():
            return all_down[chunk].reshape(D, D)

        total = jnp.zeros((1, D), f32)
        for block in range(SEQ // 512):
            total = total + feed_rows(
                pl.ds(block * 512, 512), span(chunk, D), normed_two, up_weight, down_weight, all_bias,
                low_final, hidden, grad_pre, final, grad_normed,
            )
        grad_small[pl.ds(8 + chunk, 1), :] = total
        when(0, u1.from_near)
        when(1, u1.from_far, functools.partial(down.from_far, 1))
        when(2, down_sum.to_far, up_sum.to_far)
        when(3, down_sum.pass_sum)
        weights[:, :, :, span(chunk + 2 + later * (chunk - 1), D)] = dot_tn(hidden[...], low_final[...]).astype(bf16).reshape(cut)
        when(1, down_sum.swap, u1.finish)
        when(3, up_sum.pass_sum)
        weights[:, :, :, span(chunk + later * chunk, D)] = dot_nn(normed_t[...], grad_pre[...]).astype(bf16).reshape(cut)
        when(0, functools.partial(down.from_near, 1), old_spread.finish)
        when(1, functools.partial(down.finish, 1), up_sum.swap, u1.drain)

        @pl.when(chunk >= 2)
        def _():
            for copy in chunk_copies(chunk):
                copy.start()

        return carry

    def last_copies(part):
        rows = span(part, 256)
        return (
            pltpu.make_async_copy(hidden.at[rows, :], out_tokens.at[rows, :], out_sems.at[14 + part]),
            pltpu.make_async_copy(grad_middle.at[rows, :], out_middle.at[rows, :], out_sems.at[18 + part]),
        )

    def last():
        def back(part, carry):
            gain, shift = carry
            rows = span(part, 256)
            unit, scale = normalise(middle[rows, :])
            grad = grad_normed[rows, :]
            grad_middle[rows, :] = grad_middle[rows, :] + normalise_back(grad, vec[2:3, :], unit, scale)
            hidden[rows, :] = final[rows, :].astype(bf16)
            for copy in last_copies(part):
                copy.start()
            return gain + jnp.sum(grad * unit, 0, keepdims=True), shift + jnp.sum(grad, 0, keepdims=True)

        zero = jnp.zeros((1, D), f32)
        gain, shift = lax.fori_loop(0, SEQ // 256, back, (zero, zero))
        grad_small[2:3, :] = gain
        grad_small[3:4, :] = shift
        lay_out(olds, 8, bias.shape[1], all_bias)
        moments[...] = jnp.ones_like(moments)
        lay_out(olds, 0, vectors.shape[1], moments.at[0:8, :])
        for index in range(FF // D):
            moments[8 + index : 9 + index, :] = all_bias[0:1, index * D : index * D + D]
        for index in range(ends.shape[1]):
            pooled[0, index : index + 1, :] = final[pl.ds(ends[0, index], 1), :]
        for user in (down, old_spread, up_sum, down_sum):
            user.drain()
        copies["masks"].wait()
        for part in range(4):
            for copy in last_copies(part):
                copy.wait()
        for chunk in (2, 3):
            for copy in chunk_copies(chunk):
                copy.wait()

    begin()
    spread.first()
    lay_qkv()
    g0.swap()
    g1.swap()
    g2.swap()
    lay_rest()
    u0.swap()
    down.swap()
    u1.swap()
    cotangent()
    spread.second()
    g0.own()
    g1.own()
    u0.own()
    spread.third()
    spread.fourth()
    g0.along_z()
    spread.finish()
    norm_tokens()
    g1.along_z()
    g0.from_near()
    g1.from_near()
    g2.own()
    u0.along_z()
    g0.from_far()
    down.own()
    g1.from_far()
    spread.drain()
    g0.finish()
    project_group(0)
    g1.finish()
    old_spread.first()
    attend(0, g2.along_z, old_spread.second)
    project_group(1)
    attend(1)
    g2.from_near()
    u0.from_near()
    g2.from_far()
    down.along_z(0)
    u1.own()
    g2.finish()
    project_group(2)
    attend(2)
    u0.from_far()
    old_spread.third()
    down.from_near(0)
    g0.drain()
    g1.drain()
    g2.drain()
    u0.finish()
    middle_rows()
    u1.along_z()
    down.along_z(1)
    down.from_far(0)
    old_spread.fourth()
    prepare()
    down.finish(0)
    lax.fori_loop(0, FF // D, feed, 0)
    last()


def front_call(
    mesh_shape, tokens, ends, cot_out, cot_pooled, w_qkv, w_out, w_up, w_down, vectors, bias, moment_vec, moment_bias
):
    shape = jax.ShapeDtypeStruct
    line = mesh_shape["dp"] // 2
    rows, tall = w_up.shape[0], w_down.shape[0]
    low, full = pltpu.VMEM((SEQ, D), bf16), pltpu.VMEM((SEQ, D), f32)
    dma = pltpu.SemaphoreType.DMA
    return pl.pallas_call(
        functools.partial(front_kernel, mesh_shape),
        out_shape=(
            shape((line, 2, 4 * rows, 4 * D), bf16),
            shape((SEQ, D), bf16),
            shape((SEQ, 3 * D), bf16),
            shape((SEQ, D), bf16),
            shape((SEQ, D), bf16),
            shape((SEQ, D), f32),
            shape((line, 2, 4 * rows, 2 * D), bf16),
            shape((4, 2, tall, 2 * D), bf16),
            shape((SEQ // QUERIES, WINDOW, GROUP * QUERIES), f32),
            shape((8, D), f32),
            shape((16, D), f32),
            shape((1, ends.shape[1], D), f32),
            shape((16, D), f32),
            shape((line, 2 * rows, D), bf16),
            shape((line, 2 * rows, D), f32),
            shape((2, tall, D), bf16),
            shape((2, tall, D), f32),
        ),
        in_specs=vmem(1) + [SMEM] + vmem(10),
        out_specs=tuple([pl.BlockSpec(memory_space=pl.ANY)] * 9 + vmem(8)),
        scratch_shapes=[
            pltpu.VMEM((rows, 8 * D), f32),
            pltpu.VMEM((2 * rows, 4 * D), f32),
            pltpu.VMEM((2 * tall, D // 2), f32),
            pltpu.VMEM((line, 2, 4 * rows, 8 * D), bf16),
            pltpu.VMEM((line, 2, 4 * tall, D), bf16),
            pltpu.VMEM((line, 2, 2, 2, 16, 128), bf16),
            pltpu.VMEM((line, 2, 2, 2, 16, 128), f32),
            pltpu.VMEM((1, FF), f32),
            low,
            pltpu.VMEM((SEQ, 3 * D), bf16),
            low,
            full,
            low,
            full,
            full,
            full,
            pltpu.VMEM((D, SEQ), bf16),
            pltpu.VMEM((2, SEQ // QUERIES, GROUP * QUERIES), jnp.int32),
            pltpu.VMEM((SEQ // QUERIES, WINDOW, GROUP * QUERIES), f32),
            pltpu.VMEM((96, D), bf16),
            pltpu.VMEM((line, 2, 4 * rows, D), bf16),
            pltpu.VMEM((2, line, 2 * rows, D), bf16),
            pltpu.VMEM((2, line, 2 * rows, D), bf16),
            pltpu.VMEM((4, 2, tall, D), bf16),
            pltpu.VMEM((2, 2, tall, D), bf16),
            pltpu.VMEM((2, 2, tall, D), bf16),
            dma((6, 3 * line)),
            dma((6, 3 * line)),
            dma((2, 3)),
            dma((2, 3)),
            dma((line + 3,)),
            dma((line + 3,)),
            dma((line + 3,)),
            dma((line + 3,)),
            dma((22,)),
        ],
        compiler_params=pltpu.CompilerParams(
            vmem_limit_bytes=FRONT_LIMIT, collective_id=0, has_side_effects=True
        ),
        name="front",
    )(tokens, ends, cot_out, cot_pooled, w_qkv, w_out, w_up, w_down, vectors, bias, moment_vec, moment_bias)


FRONT_LIMIT = 62 * 1024 * 1024


def attend_group_back(tile, group, proj, masks, grad_mixed):
    start = window_start(tile)
    rows, window, at = span(tile, QUERIES), pl.ds(start, WINDOW), group * D
    mask = masks[tile]
    queries = split_heads(scaled(proj[rows, at : at + WIDE]))
    grads = split_heads(grad_mixed[rows, group * WIDE : (group + 1) * WIDE])
    keys = proj[window, at + WIDE : at + 2 * WIDE]
    values = proj[window, at + 2 * WIDE : at + D]
    probs = probabilities(keys, queries, mask)
    grad_probs = dot_nt(values, grads)
    along = jnp.sum(probs * grad_probs, 0, keepdims=True)
    grad_scores = (probs * (grad_probs - along)).astype(bf16)
    both = join_heads(dot_tn(grad_scores, keys)) * HEAD_DIM ** (-0.5)
    return rows, window, both.astype(bf16), dot_nn(grad_scores, queries), dot_nn(probs.astype(bf16), grads)


def rear_kernel(mesh_shape, *refs):
    refs = list(refs)

    def take(count):
        taken = refs[:count]
        del refs[:count]
        return taken

    from_tokens, ends, from_both, vec, moments, small = take(6)
    from_proj, from_normed, from_mixed, from_middle, from_up, from_down, from_masks = take(7)
    near_up, own_up, near_down, own_down = take(4)
    weights, (vectors, bias), rows = take(4), take(2), take(4)
    out_tokens, grads, (grad_vec, grad_bias, stats) = take(1)[0], take(4), take(3)
    proj, spare, turned, low_middle, grad_mixed, grad_keys, grad_values, grad_middle, masks, w_both, tokens = take(11)
    term_out, term_groups, part_out, part_groups = take(4)
    up_rest, down_rest = take(4), take(4)
    up_mine, up_scratch, down_mine, down_scratch = take(1)[0], take(8), take(1)[0], take(8)
    scratch = take(8)
    early, late, send, recv, sems, load_sems = take(5), take(5), *take(4)
    place = Place(mesh_shape)
    line = place.line
    cut = (line, 2, D // (2 * line), D)
    def load(index, source, target):
        size = target.shape[0] // 4
        return [
            pltpu.make_async_copy(source.at[pl.ds(part * size, size)], target.at[pl.ds(part * size, size)], load_sems.at[index, part])
            for part in range(4)
        ]

    def wait_for(index):
        for copy in loads[index]:
            copy.wait()

    out_part, qkv_part = slice(3 * D, 4 * D), slice(0, 3 * D)
    loads = [
        load(0, from_middle, grad_middle),
        load(1, from_both.at[:, :, :, out_part], w_both.at[:, :, :, out_part]),
        load(2, from_mixed, spare),
        load(3, from_proj, proj),
        load(4, from_masks, masks),
        load(5, from_both.at[:, :, :, qkv_part], w_both.at[:, :, :, qkv_part]),
        load(6, from_tokens, tokens),
    ]
    normed_copy = pltpu.make_async_copy(from_normed, spare, sems.at[0])
    token_copies = [
        pltpu.make_async_copy(grad_middle.at[at : at + 512, :], out_tokens.at[at : at + 512, :], sems.at[1 + at // 512])
        for at in range(0, SEQ, 512)
    ]

    half_up = grads[2].at[:, 0 : 2 * D], grads[2].at[:, 2 * D :]
    u0 = ReduceRest(place, near_up, own_up, *up_rest, half_up[0], send.at[0], recv.at[0])
    d0 = ReducePlanesRest(place, 0, near_down, own_down, *down_rest, grads[3], send.at[1], recv.at[1])
    u1 = Reduce(place, from_up, *[ref.at[0] for ref in up_scratch], half_up[1], send.at[2], recv.at[2], up_mine)
    d1 = ReducePlanes(
        place, 2, from_down, *[ref.at[0] for ref in down_scratch], grads[3], send.at[3], recv.at[3], down_mine
    )

    def attention_of(index):
        term, part = (term_groups.at[index], part_groups.at[index]) if index < 3 else (term_out, part_out)
        return Reduce(place, term, *[ref.at[index] for ref in scratch], part, send.at[4 + index], recv.at[4 + index])

    g0, g1, g2, out = (attention_of(index) for index in range(4))
    early_sum, late_sum = AllSum(place, *early), AllSum(place, *late)
    first, second = early[0], late[0]
    local = LocalTerms(weights, rows)

    def begin():
        for copies in loads:
            for copy in copies:
                copy.start()
        greet(place)

    def prepare():
        first[...] = jnp.zeros_like(first)
        first[0:16, :] = small[...]
        second[...] = jnp.zeros_like(second)
        wait_for(0)
        wait_for(1)

    def out_back():
        w_out = w_both.at[:, :, :, 3 * D :]

        def out_part(part, total):
            return out_back_part(part, grad_middle, w_out, low_middle, grad_mixed, total)

        first[6:7, :] = lax.fori_loop(0, SEQ // 512, out_part, jnp.zeros((1, D), f32))

    def out_grad():
        wait_for(2)
        turned[...] = spare[...].T
        normed_copy.start()

        def third(part, carry):
            term = dot_nn(turned[...], low_middle[:, span(part, WIDE)]).astype(bf16)
            term_out[:, :, :, span(part, WIDE)] = term.reshape(cut[:3] + (WIDE,))
            return carry

        lax.fori_loop(0, 3, third, 0)
        normed_copy.wait()
        turned[...] = spare[...].T
        wait_for(3)
        wait_for(4)

    def tiles(group, *calls):
        at = group * D
        each = SEQ // QUERIES // 4
        grad_keys[...] = jnp.zeros_like(grad_keys)
        grad_values[...] = jnp.zeros_like(grad_values)

        def tile(index, carry):
            done = [attend_group_back(4 * index + inner, group, proj, masks, grad_mixed) for inner in range(4)]
            for where, window, query, key, value in done:
                proj[where, at : at + WIDE] = query
                grad_keys[window, :] += key
                grad_values[window, :] += value

            @pl.when(index == each // 2 - 1)
            def _():
                for call in calls:
                    call()

            return carry

        lax.fori_loop(0, each, tile, 0)

    def group_grad(group):
        at = group * D
        here = slice(group * WIDE, (group + 1) * WIDE)
        proj[:, at + WIDE : at + 2 * WIDE] = grad_keys[...].astype(bf16)
        proj[:, at + 2 * WIDE : at + D] = grad_values[...].astype(bf16)

        def third(part, carry):
            term = dot_nn(turned[...], proj[:, span(3 * group + part, WIDE)]).astype(bf16)
            term_groups[group, :, :, :, span(part, WIDE)] = term.reshape(cut[:3] + (WIDE,))
            return carry

        lax.fori_loop(0, 3, third, 0)
        first[4:5, here] = jnp.sum(proj[:, at : at + WIDE].astype(f32), 0, keepdims=True)
        first[5:6, here] = jnp.sum(proj[:, at + 2 * WIDE : at + D].astype(f32), 0, keepdims=True)

    def tokens_part(part):
        if part == 0:
            wait_for(5)
            wait_for(6)

        def quarter(index, carry):
            where = span(2 * part + index, 256)
            grad = dot_nt(proj[where, :], w_both[:, :, :, 0 : 3 * D].reshape(D, 3 * D))
            unit, scale = normalise(tokens[where, :].astype(f32))
            grad_middle[where, :] = grad_middle[where, :] + normalise_back(grad, vec[0:1, :], unit, scale)
            second[0:1, :] = second[0:1, :] + jnp.sum(grad * unit, 0, keepdims=True)
            second[1:2, :] = second[1:2, :] + jnp.sum(grad, 0, keepdims=True)
            return carry

        lax.fori_loop(0, 2, quarter, 0)
        token_copies[part].start()

    def feed_terms():
        local.matrix(2, grads[2], first, 16)
        local.matrix(3, grads[3], first, 24)
        local.rest(vectors, bias)
        first[26:27, :] = local.sums

    def out_terms():
        grads[1][...] = part_out[...]
        local.matrix(1, grads[1], first, 27)

    def qkv_terms():
        for index in range(3):
            for piece in range(3):
                at = piece * D + index * WIDE
                grads[0][:, at : at + WIDE] = part_groups[index, :, piece * WIDE : (piece + 1) * WIDE]
        local.matrix(0, grads[0], second, 2)

    def last():
        first[0:2, :] = second[0:2, :]
        grad_vec[...] = own_vectors(place, first, vectors.shape[1])
        grad_bias[...] = own_bias(place, first, bias.shape[1])
        grad = first[0:16, :]
        update = grad * lax.rsqrt(moment_of(grad, moments[...]))
        lane = lax.broadcasted_iota(jnp.int32, (1, D), 1)
        stats[...] = jnp.zeros_like(stats)
        stats[0:3, :] = second[2:5, :]
        stats[3:4, :] = first[27:28, :]
        stats[4:8, :] = first[16:20, :]
        stats[8:9, :] = first[24:25, :]
        stats[9:12, :] = second[5:8, :]
        stats[12:13, :] = first[28:29, :]
        stats[13:17, :] = first[20:24, :]
        stats[17:18, :] = first[25:26, :]
        stats[18:19, :] = jnp.where(lane == 17, total(update * update), first[26:27, :])
        for copy in token_copies:
            copy.wait()

    begin()
    u1.swap()
    u0.to_near()
    d0.to_near()
    prepare()
    out_back()
    u1.to_far()
    out_grad()
    out.swap()
    tiles(0, u0.to_line, out.to_far, d0.to_line, d1.swap)
    u1.to_near()
    out.to_near()
    d1.to_far()
    group_grad(0)
    tiles(1, u0.to_owner)
    u0.finish()
    out.to_line()
    u1.to_line()
    g0.swap()
    group_grad(1)
    g1.swap()
    d1.to_near()
    tiles(2, g0.to_far, g1.to_far, d1.to_line, d1.to_owner, d1.finish)
    out.to_owner()
    d0.to_owner()
    u1.to_owner()
    d0.finish()
    group_grad(2)
    g0.to_near()
    out.finish()
    g1.to_near()
    g2.swap()
    out_terms()
    u1.finish()
    feed_terms()
    g2.to_far()
    early_sum.start(0)
    g0.to_line()
    g1.to_line()
    tokens_part(0)
    g2.to_near()
    early_sum.next(0)
    tokens_part(1)
    g0.to_owner()
    g1.to_owner()
    early_sum.next(1)
    g2.to_line()
    g0.finish()
    g1.finish()
    early_sum.next(2)
    g2.to_owner()
    g2.finish()
    qkv_terms()
    late_sum.start(0)
    u0.drain()
    d0.drain()
    u1.drain()
    late_sum.next(0)
    d1.drain()
    out.drain()
    late_sum.next(1)
    g0.drain()
    g1.drain()
    late_sum.next(2)
    g2.drain()
    late_sum.end_line()
    early_sum.end_line()
    last()


class LocalTerms:
    def __init__(self, weights, rows):
        self.weights, self.rows = weights, rows
        self.lane = lax.broadcasted_iota(jnp.int32, (1, D), 1)
        self.sums = jnp.zeros((1, D), f32)

    def matrix(self, index, source, value, at):
        grad = source[...]
        row = row_statistic(grad, self.rows[index][...])
        square = grad * grad
        line = jnp.sum(square + square_eps, 0, keepdims=True)
        weighed = jnp.sum(square * (1.0 / row), 0, keepdims=True)
        count = grad.shape[1] // D
        for part in range(count):
            value[at + part : at + part + 1, :] = line[:, part * D : part * D + D]
            value[at + count + part : at + count + part + 1, :] = weighed[:, part * D : part * D + D]

    def rest(self, vectors, bias):
        for index in range(4):
            weight = self.weights[index][...]
            old = jnp.sum(self.rows[index][...], 1, keepdims=True)
            self.sums = jnp.where(self.lane == index, old, self.sums)
            self.sums = jnp.where(self.lane == 4 + index, total(weight * weight), self.sums)
        squares = jnp.sum(vectors[...] * vectors[...], 1, keepdims=True)
        for index in range(8):
            self.sums = jnp.where(self.lane == 8 + index, squares[index : index + 1, :], self.sums)
        self.sums = jnp.where(self.lane == 16, total(bias[...] * bias[...]), self.sums)


def rear_call(
    mesh_shape, tokens, ends, w_both, vec, moments, small, proj, normed, mixed, middle, terms, sums, weights, vectors, bias, rows
):
    shape = jax.ShapeDtypeStruct
    line = mesh_shape["dp"] // 2
    low = pltpu.VMEM((SEQ, D), bf16)
    tall, deep = weights[2].shape[0], weights[3].shape[0]
    cut = (line, 2, 4 * tall)
    far = pl.BlockSpec(memory_space=pl.ANY)
    return pl.pallas_call(
        functools.partial(rear_kernel, mesh_shape),
        out_shape=(shape((SEQ, D), f32),)
        + tuple(shape(w.shape, f32) for w in weights)
        + (shape(vectors.shape, f32), shape(bias.shape, f32), shape((24, D), f32)),
        in_specs=[far, SMEM, far] + vmem(3) + [far] * 7 + vmem(14),
        out_specs=tuple([pl.BlockSpec(memory_space=pl.ANY)] + vmem(7)),
        scratch_shapes=[
            pltpu.VMEM((SEQ, 3 * D), bf16),
            low,
            pltpu.VMEM((D, SEQ), bf16),
            low,
            low,
            pltpu.VMEM((SEQ, WIDE), f32),
            pltpu.VMEM((SEQ, WIDE), f32),
            pltpu.VMEM((SEQ, D), f32),
            pltpu.VMEM((SEQ // QUERIES, WINDOW, GROUP * QUERIES), f32),
            pltpu.VMEM(w_both.shape, bf16),
            low,
            pltpu.VMEM(cut + (D,), bf16),
            pltpu.VMEM((3,) + cut + (D,), bf16),
            pltpu.VMEM((tall, D), f32),
            pltpu.VMEM((3, tall, D), f32),
            pltpu.VMEM((line, 2 * tall, D), bf16),
            pltpu.VMEM((line - 1, 2 * tall, D), bf16),
            pltpu.VMEM((line - 1, 2 * tall, D), bf16),
            pltpu.VMEM((2 * tall, D), f32),
            pltpu.VMEM((2, deep, D), bf16),
            pltpu.VMEM((2, deep, D), bf16),
            pltpu.VMEM((line - 1, 2, deep, D), bf16),
            pltpu.VMEM((2, deep, D), f32),
            pltpu.VMEM(cut + (D,), bf16),
        ]
        + reduce_scratch(line, 2 * tall, D, 1)
        + [pltpu.VMEM((4, 2, deep, D), bf16)]
        + plane_scratch(line, deep, D, 1)
        + reduce_scratch(line, 2 * tall, D // 2, 4)
        + sum_scratch(line, 32)
        + sum_scratch(line, 8)
        + [pltpu.SemaphoreType.DMA((8, 5 + line))] * 2
        + [pltpu.SemaphoreType.DMA((3,)), pltpu.SemaphoreType.DMA((7, 4))],
        compiler_params=pltpu.CompilerParams(
            vmem_limit_bytes=FRONT_LIMIT, collective_id=1, has_side_effects=True
        ),
        name="rear",
    )(tokens, ends, w_both, vec, moments, small, proj, normed, mixed, middle, *terms, *sums, *weights, vectors, bias, *rows)


def plain_device(
    tokens,
    ends,
    cot_out,
    cot_pooled,
    w_qkv,
    w_out,
    w_up,
    w_down,
    vectors,
    bias_up,
    row_qkv,
    col_qkv,
    row_out,
    col_out,
    row_up,
    col_up,
    row_down,
    col_down,
    moment_vectors,
    moment_bias_up,
):
    low_qkv = w_qkv.astype(jnp.bfloat16)
    low_out = w_out.astype(jnp.bfloat16)
    low_up = w_up.astype(jnp.bfloat16)
    low_down = w_down.astype(jnp.bfloat16)
    low_vec = vectors.astype(jnp.bfloat16)
    low_upbias = bias_up.astype(jnp.bfloat16)
    gathered = (
        lax.all_gather(low_qkv, ("dp", "fsdp"), axis=0, tiled=True),
        lax.all_gather(low_out, ("dp", "fsdp"), axis=0, tiled=True),
        lax.all_gather(low_up, ("dp", "fsdp"), axis=0, tiled=True),
        lax.all_gather(low_down, ("dp", "fsdp"), axis=0, tiled=True),
        lax.all_gather(low_vec, ("dp", "fsdp"), axis=0, tiled=True),
        lax.all_gather(low_upbias, ("dp", "fsdp"), axis=0, tiled=True),
    )
    qkv_full, out_full, up_full, down_full = (gathered[0], gathered[1], gathered[2], gathered[3])
    vec_full = gathered[4].astype(jnp.float32)
    upbias_full = gathered[5].astype(jnp.float32)
    vec = vec_full.T
    bias = upbias_full.reshape(1, FF)
    normed, proj, mixed, middle, normed_two = forward_call(tokens, ends, qkv_full, out_full, vec)
    out_tokens, pooled, grad_middle, grad_w_up, grad_w_down, small = feed_call(
        normed_two, middle, up_full, down_full, vec, bias, cot_out, cot_pooled, ends
    )
    grad_tokens, grad_w_qkv, grad_w_out, small = backward_call(
        tokens, ends, qkv_full, out_full, vec, normed, proj, mixed, grad_middle, small
    )
    grad_vectors = small[:8].T
    grad_bias_up = small[8:12].reshape(FF)
    summed_up, summed_down, summed_upbias = (
        lax.psum_scatter(grad_w_up.astype(f32), ("dp", "fsdp"), scatter_dimension=0, tiled=True),
        lax.psum_scatter(grad_w_down.astype(f32), ("dp", "fsdp"), scatter_dimension=0, tiled=True),
        lax.psum_scatter(grad_bias_up, ("dp", "fsdp"), scatter_dimension=0, tiled=True),
    )
    summed_qkv, summed_out, summed_vec = (
        lax.psum_scatter(grad_w_qkv.astype(f32), ("dp", "fsdp"), scatter_dimension=0, tiled=True),
        lax.psum_scatter(grad_w_out.astype(f32), ("dp", "fsdp"), scatter_dimension=0, tiled=True),
        lax.psum_scatter(grad_vectors, ("dp", "fsdp"), scatter_dimension=0, tiled=True),
    )
    matrices = (summed_qkv, summed_out, summed_up, summed_down)
    old_rows = (row_qkv, row_out, row_up, row_down)
    old_cols = (col_qkv, col_out, col_up, col_down)
    masters = (w_qkv, w_out, w_up, w_down)
    row_sizes = (D, D, D, FF)
    tensor_sizes = (3 * D * D, D * D, D * FF, FF * D)
    squares = [gradient * gradient + square_eps for gradient in matrices]
    rows_new = [
        decay * old + (1.0 - decay) * jnp.mean(square, 1) for old, square in zip(old_rows, squares)
    ]
    col_parts = [jnp.sum(square, 0) for square in squares]
    local_totals = jnp.concatenate(
        [
            jnp.stack([jnp.sum(renewed) for renewed in rows_new]),
            jnp.stack([jnp.sum(master * master) for master in masters]),
            jnp.sum(vectors * vectors, 0),
            jnp.sum(bias_up * bias_up)[None],
        ]
    )
    col_sum_qkv, col_sum_out, col_sum_up, col_sum_down, global_totals = lax.psum(
        (col_parts[0], col_parts[1], col_parts[2], col_parts[3], local_totals), ("dp", "fsdp")
    )
    col_sums = (col_sum_qkv, col_sum_out, col_sum_up, col_sum_down)
    cols_new = [
        decay * old + (1.0 - decay) * (summed / count)
        for old, summed, count in zip(old_cols, col_sums, row_sizes)
    ]
    updates = []
    for index_mat in range(4):
        row_mean = global_totals[index_mat] / row_sizes[index_mat]
        renewed_row = rows_new[index_mat]
        renewed_col = cols_new[index_mat]
        updates.append(
            matrices[index_mat] * lax.rsqrt(renewed_row[:, None] * renewed_col[None, :] / row_mean)
        )
    moment_vec = decay * moment_vectors + (1.0 - decay) * (summed_vec * summed_vec + square_eps)
    update_vec = summed_vec * lax.rsqrt(moment_vec)
    moment_upb = decay * moment_bias_up + (1.0 - decay) * (
        summed_upbias * summed_upbias + square_eps
    )
    update_upb = summed_upbias * lax.rsqrt(moment_upb)
    local_norm = jnp.sum(update_vec * update_vec) + jnp.sum(update_upb * update_upb)
    for update in updates:
        local_norm = local_norm + jnp.sum(update * update)
    norm_total = lax.psum(local_norm, ("dp", "fsdp"))
    param_count = 4 * D * D + 2 * D * FF + 8 * D + FF
    clip = jnp.maximum(1.0, jnp.sqrt(norm_total / param_count) / clip_limit)
    new_weights = []
    for index_mat in range(4):
        scale = jnp.maximum(
            scale_floor, jnp.sqrt(global_totals[4 + index_mat] / tensor_sizes[index_mat])
        )
        new_weights.append(masters[index_mat] - step_rate * scale * updates[index_mat] / clip)
    vec_scale = jnp.maximum(scale_floor, jnp.sqrt(global_totals[8:16] / D))[None, :]
    new_vec = vectors - step_rate * vec_scale * update_vec / clip
    upb_scale = jnp.maximum(scale_floor, jnp.sqrt(global_totals[16] / FF))
    new_upb = bias_up - step_rate * upb_scale * update_upb / clip
    return (
        out_tokens,
        pooled,
        grad_tokens,
        summed_qkv,
        rows_new[0],
        cols_new[0],
        new_weights[0],
        summed_out,
        rows_new[1],
        cols_new[1],
        new_weights[1],
        summed_up,
        rows_new[2],
        cols_new[2],
        new_weights[2],
        summed_down,
        rows_new[3],
        cols_new[3],
        new_weights[3],
        summed_vec,
        moment_vec,
        new_vec,
        summed_upbias,
        moment_upb,
        new_upb,
        clip,
    )


def kernels_fit(mesh_shape):
    rows = D // (mesh_shape["dp"] * mesh_shape["fsdp"])
    return mesh_shape["fsdp"] == 4 and mesh_shape["dp"] == 8 and rows % 8 == 0


def per_device(
    mesh_shape,
    tokens,
    ends,
    cot_out,
    cot_pooled,
    w_qkv,
    w_out,
    w_up,
    w_down,
    vectors,
    bias_up,
    row_qkv,
    col_qkv,
    row_out,
    col_out,
    row_up,
    col_up,
    row_down,
    col_down,
    moment_vectors,
    moment_bias_up,
):
    def whole(array):
        return array.reshape(-1, array.shape[-1])

    def row(array):
        return array.reshape(1, -1)

    bias_row = row(bias_up)
    moments = (moment_vectors.T, row(moment_bias_up))
    both, normed, proj, mixed, out_tokens, grad_middle, *terms, vec, all_moments, pooled, small, a, b, e, f = front_call(
        mesh_shape, tokens, ends, cot_out, cot_pooled, w_qkv, w_out, w_up, w_down, vectors.T, bias_row, *moments
    )
    weights = (w_qkv, w_out, w_up, w_down)
    rows = [row(value) for value in (row_qkv, row_out, row_up, row_down)]
    cols = [col_qkv, col_out, col_up, col_down]
    grad_tokens, *summed = rear_call(
        mesh_shape, tokens, ends, both, vec, all_moments, small, proj, normed, mixed, grad_middle,
        terms, (a, b, e, f), weights, vectors.T, bias_row, rows
    )
    large = (out_tokens, pooled, grad_tokens)
    done = finish_call(large, summed, weights, vectors.T, bias_row, rows, cols, *moments)
    results, done = list(done[:3]), done[3:]
    for index in range(4):
        results += [done[index], done[4 + index].reshape(-1), done[8 + index], done[12 + index]]
    results += [value.T for value in done[16:19]] + [value.reshape(-1) for value in done[19:22]]
    return tuple(results + [done[22].reshape(())])


def solution(mesh):
    in_specs = (
        P(("dp", "fsdp"), None),
        P(("dp", "fsdp"), None),
        P(("dp", "fsdp"), None),
        P(("dp", "fsdp"), None, None),
        P(("dp", "fsdp"), None),
        P(("dp", "fsdp"), None),
        P(("dp", "fsdp"), None),
        P(("dp", "fsdp"), None),
        P(("dp", "fsdp"), None),
        P(("dp", "fsdp")),
        P(("dp", "fsdp")),
        P(),
        P(("dp", "fsdp")),
        P(),
        P(("dp", "fsdp")),
        P(),
        P(("dp", "fsdp")),
        P(),
        P(("dp", "fsdp"), None),
        P(("dp", "fsdp")),
    )
    out_specs = (
        P(("dp", "fsdp"), None),
        P(("dp", "fsdp"), None, None),
        P(("dp", "fsdp"), None),
        P(("dp", "fsdp"), None),
        P(("dp", "fsdp")),
        P(),
        P(("dp", "fsdp"), None),
        P(("dp", "fsdp"), None),
        P(("dp", "fsdp")),
        P(),
        P(("dp", "fsdp"), None),
        P(("dp", "fsdp"), None),
        P(("dp", "fsdp")),
        P(),
        P(("dp", "fsdp"), None),
        P(("dp", "fsdp"), None),
        P(("dp", "fsdp")),
        P(),
        P(("dp", "fsdp"), None),
        P(("dp", "fsdp"), None),
        P(("dp", "fsdp"), None),
        P(("dp", "fsdp"), None),
        P(("dp", "fsdp")),
        P(("dp", "fsdp")),
        P(("dp", "fsdp")),
        P(),
    )
    fits = kernels_fit(mesh.shape)
    step = functools.partial(per_device, dict(mesh.shape)) if fits else plain_device
    return jax.shard_map(
        step, mesh=mesh, in_specs=in_specs, out_specs=out_specs, check_vma=False
    )
```

time: 1030 us -> 230 us (0.22); the launches traced: 1020 us -> 230 us
  waiting for transfers between devices: 432 us -> 0 us
  matrix products: 247 us -> 0 us
  Pallas kernels: 0 us -> 229 us
  blocking collectives: 164 us -> 0 us
  other arithmetic: 98.1 us -> 0 us
  local copies, waits for them, and re-layouts: 50 us -> 0 us
  between operations: 27.2 us -> 0.88 us
    reduce_scatter x4 -> x0, waiting for transfers between devices: 379 us -> none  [the longest x1 140 us: per_device(): lax.psum_scatter(grad_w_up, ('dp', 'fsdp'), scatter_dimension=0, tiled=True)]
    pallas_call x0 -> x3, Pallas kernels: none -> 229 us  [the longest x1 119 us: front_call(): pl.pallas_call(functools.partial(front_kernel, mesh_shape), out_shape=(sh...]
    dot_general x24 -> x0, matrix products: 217 us -> none  [the longest x2 37.8 us: attend_back(): jnp.einsum('qhd,khd->hqk', grad_block, value_heads, preferred_element_typ...]
    psum x2 -> x0, blocking collectives: 80.8 us -> none  [the longest x1 41.5 us: per_device(): lax.psum((col_parts[0], col_parts[1], col_parts[2], col_parts[3], local_t...]
    all_gather x4 -> x0, waiting for transfers between devices: 52.7 us -> none  [the longest x1 52.7 us: per_device(): lax.all_gather(low_down, ('dp', 'fsdp'), axis=0, tiled=True)]
    reduce_sum x31 -> x0, other arithmetic: 44.5 us -> none  [the longest x4 9.32 us: per_device(): jnp.sum(master * master)]
    unnamed x1 -> x0, blocking collectives: 42.6 us -> none
    all_gather x1 -> x0, blocking collectives: 40.1 us -> none  [per_device(): lax.all_gather(low_vec, ('dp', 'fsdp'), axis=0, tiled=True)]
  transfers between devices with their start and end apart: 8 -> 0, of which waited for: 4 -> 0; matrix products, arithmetic and copies ran while one was open for 23% -> 0% of each run, Pallas kernels for 0% -> 0%
where the time goes in v1:
time: 230 us
  Pallas kernels  229 us (100%)
    pallas_call x1, Pallas kernels, front_call(): pl.pallas_call(functools.partial(front_kernel, mesh_shape), out_shape=(sh...  119 us
    pallas_call x1, Pallas kernels, rear_call(): pl.pallas_call(functools.partial(rear_kernel, mesh_shape), out_shape=(sha...  102 us
    pallas_call x1, Pallas kernels, finish_call(): pl.pallas_call(finish_kernel, out_shape=tuple([shape(value.shape, value.d...  7.87 us

profile of v1, /device:TPU:0, one launch (start us, length us, event | category | flops | bytes accessed | tf_op | source)
XLA Modules:
  0.0 229.5 jit_solution(14237083488663859616)
XLA Ops:
  0.7 118.9 %front.1 = (bf16[4,2,96,3072]{3,2,1,0:T(8,128)(2,1)}, bf16[1024,768]{1,0:T(8,128)(2,1)}, bf16[1024,2304]{1,0:T(8,128)(2,1)}, bf16[1024,768]{1,0:T(8,128)(2,1)}, ...) custom-call(bf16[1024,768]{1,0:T(8,128)(2,1)} %refs_0_.3, ...), custom_call_target="tpu_custom_call" | custom-call | tf_op jit(solution)/shard_map/front/pallas_call | solution.py:1670
  119.6 101.9 %rear.1 = (f32[1024,768]{1,0:T(8,128)}, f32[24,2304]{1,0:T(8,128)}, f32[24,768]{1,0:T(8,128)}, f32[24,3072]{1,0:T(8,128)}, f32[96,768]{1,0:T(8,128)}, /*index=5*...) custom-call(bf16[1024,768]{1,0:T(8,128)(2,1)} %refs_0_.3, s32[1,24]{1,0:T(1,128)} %refs_1_.3, ...), custom_call_target="tpu_custom_call" | custom-call | tf_op jit(solution)/shard_map/rear/pallas_call | solution.py:2058
  221.5 7.9 %finish.1 = (bf16[1024,768]{1,0:T(8,128)(2,1)}, f32[1,24,768]{2,1,0:T(8,128)}, f32[1024,768]{1,0:T(8,128)}, f32[24,2304]{1,0:T(8,128)}, f32[24,768]{1,0:T(8,128)...) custom-call(bf16[1024,768]{1,0:T(8,128)(2,1)} %get-tuple-element.77., ...), custom_call_target="tpu_custom_call" | custom-call | tf_op jit(solution)/shard_map/finish/pallas_call | solution.py:1310

commit v2 on v1

--- a/solution.py
+++ b/solution.py
@@ -1187,12 +1187,12 @@
     return jnp.sum(jnp.sum(values, 1, keepdims=True), 0, keepdims=True)
 
 
-def own_vectors(place, small, size):
+def own_vectors(place, small, result, indices):
+    size = result.shape[1]
     shape = (size, D)
     pick = lax.broadcasted_iota(jnp.int32, shape, 1) == place.flat * size + lax.broadcasted_iota(jnp.int32, shape, 0)
     row = lax.broadcasted_iota(jnp.int32, (8, size), 0)
-    result = jnp.zeros((8, size), f32)
-    for index in range(8):
+    for index in indices:
         column = jnp.sum(jnp.where(pick, small[index : index + 1, :], 0.0), 1, keepdims=True)
         result = jnp.where(row == index, to_row(column), result)
     return result
@@ -1237,7 +1237,7 @@
     out_vec, new_moment_vec, new_vec, out_bias, new_moment_bias, new_bias, clip_out = take(7)
     held, sems = take(3), take(1)[0]
     copies = []
-    for index, count in enumerate((4, 1, 8)):
+    for index, count in enumerate((1, 1, 1)):
         size = held[index].shape[0] // count
         for part in range(count):
             piece, at = pl.ds(part * size, size), len(copies)
@@ -1319,7 +1319,7 @@
         ),
         in_specs=[pl.BlockSpec(memory_space=pl.ANY)] * 3 + vmem(23),
         out_specs=tuple([pl.BlockSpec(memory_space=pl.ANY)] * 3 + vmem(23)),
-        scratch_shapes=[pltpu.VMEM(value.shape, value.dtype) for value in large] + [pltpu.SemaphoreType.DMA((2, 13))],
+        scratch_shapes=[pltpu.VMEM(value.shape, value.dtype) for value in large] + [pltpu.SemaphoreType.DMA((2, 3))],
         compiler_params=pltpu.CompilerParams(vmem_limit_bytes=VMEM_LIMIT),
         name="finish",
     )(*large, *summed, *weights, vectors, bias, *rows, *cols, moment_vec, moment_bias)
@@ -1927,23 +1927,31 @@
                 grads[0][:, at : at + WIDE] = part_groups[index, :, piece * WIDE : (piece + 1) * WIDE]
         local.matrix(0, grads[0], second, 2)
 
-    def last():
-        first[0:2, :] = second[0:2, :]
-        grad_vec[...] = own_vectors(place, first, vectors.shape[1])
+    def squared_updates(grad, moment):
+        update = grad * lax.rsqrt(moment_of(grad, moment))
+        return total(update * update)
+
+    def early_results():
+        grad_vec[...] = own_vectors(place, first, jnp.zeros(vectors.shape, f32), range(2, 8))
         grad_bias[...] = own_bias(place, first, bias.shape[1])
-        grad = first[0:16, :]
-        update = grad * lax.rsqrt(moment_of(grad, moments[...]))
-        lane = lax.broadcasted_iota(jnp.int32, (1, D), 1)
         stats[...] = jnp.zeros_like(stats)
-        stats[0:3, :] = second[2:5, :]
         stats[3:4, :] = first[27:28, :]
         stats[4:8, :] = first[16:20, :]
         stats[8:9, :] = first[24:25, :]
-        stats[9:12, :] = second[5:8, :]
         stats[12:13, :] = first[28:29, :]
         stats[13:17, :] = first[20:24, :]
         stats[17:18, :] = first[25:26, :]
-        stats[18:19, :] = jnp.where(lane == 17, total(update * update), first[26:27, :])
+        lane = lax.broadcasted_iota(jnp.int32, (1, D), 1)
+        norm = squared_updates(first[0:16, :], moments[...])
+        stats[18:19, :] = jnp.where(lane == 17, norm, first[26:27, :])
+
+    def last():
+        grad_vec[...] = own_vectors(place, second, grad_vec[...], range(2))
+        stats[0:3, :] = second[2:5, :]
+        stats[9:12, :] = second[5:8, :]
+        lane = lax.broadcasted_iota(jnp.int32, (1, D), 1)
+        norm = squared_updates(second[0:2, :], moments[0:2, :])
+        stats[18:19, :] = jnp.where(lane == 17, stats[18:19, :] + norm, stats[18:19, :])
         for copy in token_copies:
             copy.wait()
 
@@ -2010,10 +2018,11 @@
     late_sum.next(1)
     g0.drain()
     g1.drain()
+    early_sum.end_line()
     late_sum.next(2)
     g2.drain()
+    early_results()
     late_sum.end_line()
-    early_sum.end_line()
     last()
 
 

time: 230 us -> 229 us (level)
  no operation moved by 1% of the time
where the time goes in v2:
time: 229 us
  Pallas kernels  228 us (100%)
    pallas_call x1, Pallas kernels, front_call(): pl.pallas_call(functools.partial(front_kernel, mesh_shape), out_shape=(sh...  119 us
    pallas_call x1, Pallas kernels, rear_call(): pl.pallas_call(functools.partial(rear_kernel, mesh_shape), out_shape=(sha...  102 us
    pallas_call x1, Pallas kernels, finish_call(): pl.pallas_call(finish_kernel, out_shape=tuple([shape(value.shape, value.d...  7.13 us

profile of v2, /device:TPU:0, one launch (start us, length us, event | category | flops | bytes accessed | tf_op | source)
XLA Modules:
  0.0 228.7 jit_solution(1440009674837621430)
XLA Ops:
  0.7 118.9 %front.1 = (bf16[4,2,96,3072]{3,2,1,0:T(8,128)(2,1)}, bf16[1024,768]{1,0:T(8,128)(2,1)}, bf16[1024,2304]{1,0:T(8,128)(2,1)}, bf16[1024,768]{1,0:T(8,128)(2,1)}, ...) custom-call(bf16[1024,768]{1,0:T(8,128)(2,1)} %refs_0_.3, ...), custom_call_target="tpu_custom_call" | custom-call | tf_op jit(solution)/shard_map/front/pallas_call | solution.py:1670
  119.6 101.8 %rear.1 = (f32[1024,768]{1,0:T(8,128)}, f32[24,2304]{1,0:T(8,128)}, f32[24,768]{1,0:T(8,128)}, f32[24,3072]{1,0:T(8,128)}, f32[96,768]{1,0:T(8,128)}, /*index=5*...) custom-call(bf16[1024,768]{1,0:T(8,128)(2,1)} %refs_0_.3, s32[1,24]{1,0:T(1,128)} %refs_1_.3, ...), custom_call_target="tpu_custom_call" | custom-call | tf_op jit(solution)/shard_map/rear/pallas_call | solution.py:2067
  221.3 7.1 %finish.1 = (bf16[1024,768]{1,0:T(8,128)(2,1)}, f32[1,24,768]{2,1,0:T(8,128)}, f32[1024,768]{1,0:T(8,128)}, f32[24,2304]{1,0:T(8,128)}, f32[24,768]{1,0:T(8,128)...) custom-call(bf16[1024,768]{1,0:T(8,128)(2,1)} %get-tuple-element.77., ...), custom_call_target="tpu_custom_call" | custom-call | tf_op jit(solution)/shard_map/finish/pallas_call | solution.py:1310
